TPU v7x, 32 devices: a whole 2x2x4 slice. The times are simulated.
32 devices in a mesh: groups: 2 (over y), expert: 16 (over z, x, core), tensor: 1.
Axes of the slice: x: 2, y: 2, z: 4, core: 2. Of those that a mesh axis runs over, the one named last changes fastest.
Arguments:
- tokens: bfloat16 [256, 2048], P(('groups', 'expert', 'tensor')), parts along dimension 0, may hold values from -6 to 6
- routes: int32 [256, 8], P(('groups', 'expert')), parts along dimension 0, may hold values from 0 to 15, all different within a row; in each aligned block of 8 rows (0 to 7, 8 to 15, ...) at most 8 rows name the same one
- combine: float32 [256, 8], P(('groups', 'expert')), parts along dimension 0, may hold values from 0.1 to 1
- prune_mask: int32 [16, 6], P('expert', 'tensor'), may hold values 0 or 1
- gate_weight: bfloat16 [16, 2048, 768], P('expert', None, 'tensor'), may hold values from -0.125 to 0.125
- up_weight: bfloat16 [16, 2048, 768], P('expert', None, 'tensor'), may hold values from -0.125 to 0.125
- down_weight: bfloat16 [16, 768, 2048], P('expert', 'tensor'), may hold values from -0.21875 to 0.21875
Outputs:
- mixed: bfloat16 [256, 2048], P(('groups', 'expert', 'tensor')), parts along dimension 0
There are 2 independent parts, one for each index of `groups`. A program takes and returns all parts, laid end to end along the dimension named above; an argument that names none is the same for every part. Nothing has to cross between parts.
Inputs may be any that keep to these rules, and one draw needn't show every extreme that they name: `routes`: each row names 8 different experts; in each aligned block of 8 rows no expert is named by more than 8 rows. `prune_mask`: 1 keeps a block of 128 hidden units, 0 prunes it.
All inputs are finite; a program needn't handle non-finite values.
Results may differ from a plain program's by a relative error of at most 0.011.
Values may be sent and summed in bfloat16 or wider, within the bound.
No kernel may reach another device: no remote copies, remote signals or barrier semaphores. Data moves between devices by JAX's collectives and lax.ppermute only.
A program may use at most 192 MiB of HBM per device.

v0:
```python
import jax
import jax.numpy as jnp
from jax import lax
from jax.sharding import PartitionSpec as P

BLK = 128


def slot_places(group_routes, experts, capacity):
    flat_routes = group_routes.reshape(-1)
    onehot = (flat_routes[:, None] == jnp.arange(experts, dtype=jnp.int32)[None, :]).astype(
        jnp.int32
    )
    before = jnp.cumsum(onehot, axis=0) - onehot
    slot_index = jnp.sum(before * onehot, axis=1)
    return flat_routes * capacity + slot_index


def fill_slots(row_source, places, experts, capacity, top_k):
    owners = jnp.full((experts * capacity,), -1, jnp.int32)
    owners = owners.at[places].set(jnp.arange(places.shape[0], dtype=jnp.int32) // top_k)
    filled = owners >= 0
    outgoing = row_source[jnp.maximum(owners, 0)]
    outgoing = jnp.where(filled[:, None], outgoing, jnp.zeros_like(outgoing))
    return outgoing.reshape(experts, capacity, row_source.shape[1])


def expert_partial(row_block, gate_weight, up_weight, down_weight, prune_mask):
    keep_cols = jnp.repeat(prune_mask[0].astype(jnp.float32), BLK)
    gate_act = jnp.dot(row_block, gate_weight[0], preferred_element_type=jnp.float32)
    up_act = jnp.dot(row_block, up_weight[0], preferred_element_type=jnp.float32)
    hidden = (jax.nn.silu(gate_act) * up_act * keep_cols).astype(jnp.bfloat16)
    partial_value = jnp.dot(hidden, down_weight[0], preferred_element_type=jnp.float32)
    rounded = lax.optimization_barrier(partial_value.astype(jnp.bfloat16))
    return rounded.astype(jnp.float32)


def body(tokens, routes, combine, prune_mask, gate_weight, up_weight, down_weight):
    tok_dev, model_width = tokens.shape
    group_rows, top_k = routes.shape
    experts = lax.axis_size("expert")
    capacity = min(group_rows, 2 * group_rows * top_k // experts)
    places = slot_places(routes, experts, capacity)
    pair_rows = lax.all_gather(tokens, "tensor", axis=0, tiled=True)
    outgoing = fill_slots(pair_rows, places, experts, capacity, top_k)
    received = lax.all_to_all(outgoing, "expert", split_axis=0, concat_axis=0, tiled=True)
    item_count = received.shape[1]
    partial_value = expert_partial(
        received.reshape(-1, model_width), gate_weight, up_weight, down_weight, prune_mask
    )
    whole_sum = lax.psum(partial_value.astype(jnp.bfloat16), "tensor")
    answers = whole_sum.reshape(experts, item_count, model_width)
    returned = lax.all_to_all(answers, "expert", split_axis=0, concat_axis=0, tiled=True).reshape(
        -1, model_width
    )
    member = lax.axis_index("tensor")
    own_places = lax.dynamic_slice_in_dim(places, member * tok_dev * top_k, tok_dev * top_k, 0)
    own_weights = lax.dynamic_slice_in_dim(combine, member * tok_dev, tok_dev, 0)
    picked = returned[own_places].reshape(tok_dev, top_k, model_width).astype(jnp.float32)
    mixed_out = jnp.einsum("tk,tkd->td", own_weights, picked)
    return mixed_out.astype(jnp.bfloat16)


def solution(mesh):
    in_specs = (
        P(("groups", "expert", "tensor"), None),
        P(("groups", "expert"), None),
        P(("groups", "expert"), None),
        P("expert", "tensor"),
        P("expert", None, "tensor"),
        P("expert", None, "tensor"),
        P("expert", "tensor", None),
    )
    out_specs = P(("groups", "expert", "tensor"), None)
    return jax.shard_map(body, mesh=mesh, in_specs=in_specs, out_specs=out_specs, check_vma=False)
```

profile of v0, /device:TPU:0, one launch (start us, length us, event | category | flops | bytes accessed | tf_op | source)
XLA Modules:
  0.0 58.5 jit_solution(10606660244901922006)
XLA Ops:
  0.0 0.0 copy-start
  0.0 0.9 %eq.15 = s32[64]{0:T(128)S(1)} reshape(s32[8,8]{1,0:T(8,128)} %param.8) | data formatting | bytes 512 | tf_op jit(solution)/shard_map/eq | solution.py:11
  0.9 0.7 %broadcast_multiply_fusion = s32[8,8]{1,0:T(8,128)S(1)} fusion(s32[8,8]{1,0:T(8,128)} %param.8), kind=kLoop, calls=%fused_computation.33 | loop fusion | flops 64 | bytes 512 | tf_op jit(solution)/shard_map/mul | solution.py:16
  1.7 0.1 fusion.32
  1.7 0.1 reduce_window_sum.11
  1.8 0.2 select_reduce_fusion
  2.0 0.1 mul.42
  2.1 0.8 %scatter_custom_fusion = s32[128]{0:T(128)S(1)} fusion(s32[64]{0:T(128)S(1)} %fusion.33, s32[64]{0:T(128)S(1)} %and_select_fusion, s32[]{:T(128)} %constant.31.clone.1), kind=kCustom, calls=%fused_computation.43 | custom fusion | bytes 516 | tf_op jit(solution)/shard_map/scatter | solution.py:21
  2.9 0.1 broadcast_in_dim.27
  3.0 0.0 copy-start.2
  3.0 3.0 %gather_fusion = bf16[128,2048]{1,0:T(8,128)(2,1)} fusion(bf16[8,2048]{1,0:T(8,128)(2,1)} %param.7, s32[1024]{0:T(1024)S(1)} %pad_clamp_fusion.1), kind=kCustom, calls=%fused_computation | custom fusion | bytes 1049088 | tf_op jit(solution)/shard_map/gather | solution.py:23
  6.0 2.0 %bitcast_select_fusion = bf16[16,8,2048]{2,1,0:T(8,128)(2,1)} fusion(bf16[128,2048]{1,0:T(8,128)(2,1)} %gather_fusion, pred[16,8]{1,0:T(8,128)(4,1)S(1)} %broadcast_in_dim.27), kind=kLoop, calls=%fused_computation.15 | loop fusion | flops 262144 | bytes 1048704 | tf_op jit(solution)/shard_map/jit(_where)/select_n | solution.py:24
  8.0 7.4 %all-to-all-start = ((bf16[16,8,2048]{2,1,0:T(8,128)(2,1)}), bf16[16,8,2048]{2,1,0:T(8,128)(2,1)}, u32[]{:S(2)}, u32[]{:S(2)}) async-start(bf16[16,8,2048]{2,1,0:T(8,128)(2,1)} %bitcast_select_fusion), calls=%async_computation | async-start | bytes 1048576 | tf_op jit(solution)/shard_map/all_to_all | solution.py:46
  15.4 0.0 copy-done.2
  15.4 0.1 broadcast_bitcast_fusion
  15.5 14.4 %all-to-all-done = bf16[16,8,2048]{2,1,0:T(8,128)(2,1)} async-done(((bf16[16,8,2048]{2,1,0:T(8,128)(2,1)}), bf16[16,8,2048]{2,1,0:T(8,128)(2,1)}, u32[]{:S(2)}, u32[]{:S(2)}) %all-to-all-start) | async-done | bytes 524320 | tf_op jit(solution)/shard_map/all_to_all | solution.py:46
  29.9 2.6 %fusion.4 = f32[128,768]{1,0:T(8,128)S(1)} fusion(bf16[1,2048,768]{2,1,0:T(8,128)(2,1)} %param.11, bf16[16,8,2048]{2,1,0:T(8,128)(2,1)} %all-to-all-done), kind=kOutput, calls=%fused_computation.7 | convolution fusion | flops 402653184 | bytes 4063232 | tf_op jit(solution)/shard_map/dot_general | solution.py:30
  32.6 0.0 copy-done
  32.6 4.1 %fusion.6 = bf16[128,2048]{1,0:T(8,128)(2,1)} fusion(bf16[1,768,2048]{2,1,0:T(8,128)(2,1)S(1)} %copy-done, bf16[1,2048,768]{2,1,0:T(8,128)(2,1)} %param.12, bf16[16,8,2048]{2,1,0:T(8,128)(2,1)} %all-to-all-done, f32[128,768]{1,0:T(8,128)S(1)} %fusion.4, f32[768]{0:T(1024)S(1)} %broadcast_bitcast_fusion), kind=kOutput, calls=%fused_computation.9 | convolution fusion | flops 806256640 | bytes 7736320 | tf_op jit(solution)/shard_map/dot_general | solution.py:33
  36.7 0.0 copy-start.1
  36.7 4.4 %all-to-all-start.1 = ((bf16[16,8,2048]{2,1,0:T(8,128)(2,1)}), bf16[16,8,2048]{2,1,0:T(8,128)(2,1)}, u32[]{:S(2)}, u32[]{:S(2)}) async-start(bf16[16,8,2048]{2,1,0:T(8,128)(2,1)} %bitcast.49), calls=%async_computation.1 | async-start | bytes 1048576 | tf_op jit(solution)/shard_map/all_to_all | solution.py:53
  41.1 14.5 %all-to-all-done.1 = bf16[16,8,2048]{2,1,0:T(8,128)(2,1)} async-done(((bf16[16,8,2048]{2,1,0:T(8,128)(2,1)}), bf16[16,8,2048]{2,1,0:T(8,128)(2,1)}, u32[]{:S(2)}, u32[]{:S(2)}) %all-to-all-start.1) | async-done | bytes 524320 | tf_op jit(solution)/shard_map/all_to_all | solution.py:53
  55.6 2.1 %gather_fusion.1 = bf16[64,2048]{1,0:T(8,128)(2,1)S(1)} fusion(bf16[128,2048]{1,0:T(8,128)(2,1)} %bitcast.10, s32[1024]{0:T(1024)S(1)} %pad_clamp_fusion), kind=kCustom, calls=%fused_computation.1 | custom fusion | bytes 524544 | tf_op jit(solution)/shard_map/gather | solution.py:59
  57.7 0.0 copy-done.1
  57.7 0.2 fusion.28
  57.9 0.6 %copy.11 = bf16[8,1,2048]{2,0,1:T(8,128)(2,1)} copy(bf16[8,1,2048]{2,1,0:T(2,128)(2,1)S(1)} %fusion.28) | data formatting | bytes 65536 | tf_op jit(solution)/shard_map/tk,tkd->td/dot_general | solution.py:60
  (7 shorter events, 0.0 us)
Async XLA Ops:
  0.0 32.6 %copy-start = (bf16[1,768,2048]{2,1,0:T(8,128)(2,1)S(1)}, bf16[1,768,2048]{2,1,0:T(8,128)(2,1)}, u32[]{:S(2)}) copy-start(bf16[1,768,2048]{2,1,0:T(8,128)(2,1)} %param.13) | copy-start | bytes 9437188
  3.0 12.4 %copy-start.2 = (s32[1,6]{1,0:T(1,128)S(1)}, s32[1,6]{1,0:T(1,128)}, u32[]{:S(2)}) copy-start(s32[1,6]{1,0:T(1,128)} %param.10) | copy-start | bytes 76
  8.0 21.9 %all-to-all-start = ((bf16[16,8,2048]{2,1,0:T(8,128)(2,1)}), bf16[16,8,2048]{2,1,0:T(8,128)(2,1)}, u32[]{:S(2)}, u32[]{:S(2)}) async-start(bf16[16,8,2048]{2,1,0:T(8,128)(2,1)} %bitcast_select_fusion), calls=%async_computation | async-start | bytes 1048576 | tf_op jit(solution)/shard_map/all_to_all | solution.py:46
  36.7 20.9 %copy-start.1 = (f32[8,8]{1,0:T(8,128)S(1)}, f32[8,8]{1,0:T(8,128)}, u32[]{:S(2)}) copy-start(f32[8,8]{1,0:T(8,128)} %param.9) | copy-start | bytes 772
  36.7 18.8 %all-to-all-start.1 = ((bf16[16,8,2048]{2,1,0:T(8,128)(2,1)}), bf16[16,8,2048]{2,1,0:T(8,128)(2,1)}, u32[]{:S(2)}, u32[]{:S(2)}) async-start(bf16[16,8,2048]{2,1,0:T(8,128)(2,1)} %bitcast.49), calls=%async_computation.1 | async-start | bytes 1048576 | tf_op jit(solution)/shard_map/all_to_all | solution.py:53
where the time goes:
time: 59.1 us; the launch traced here: 58.5 us
  waiting for transfers between devices  28.9 us (49%)
  starting transfers between devices  11.8 us (20%)
  local copies, waits for them, and re-layouts  7.69 us (13%)
  matrix products  6.98 us (12%)
  other arithmetic  3.07 us (5%)
    all_to_all x1, waiting for transfers between devices, body(): lax.all_to_all(answers, 'expert', split_axis=0, concat_axis=0, tiled=True)  14.5 us
    all_to_all x1, waiting for transfers between devices, body(): lax.all_to_all(outgoing, 'expert', split_axis=0, concat_axis=0, tiled=True)  14.4 us
    all_to_all x1, starting transfers between devices, body(): lax.all_to_all(outgoing, 'expert', split_axis=0, concat_axis=0, tiled=True)  7.41 us
    all_to_all x1, starting transfers between devices, body(): lax.all_to_all(answers, 'expert', split_axis=0, concat_axis=0, tiled=True)  4.37 us
    dot_general x1, matrix products, expert_partial(): jnp.dot(hidden, down_weight[0], preferred_element_type=jnp.float32)  4.14 us
    gather x1, local copies, waits for them, and re-layouts, fill_slots(): outgoing = row_source[jnp.maximum(owners, 0)]  3 us
    dot_general x1, matrix products, expert_partial(): jnp.dot(row_block, gate_weight[0], preferred_element_type=jnp.float32)  2.63 us
    gather x1, local copies, waits for them, and re-layouts, body(): returned[own_places].reshape(tok_dev, top_k, model_width)  2.1 us
  transfers between devices with their start and end apart: 2, of which 2 were waited for; matrix products, arithmetic and copies ran while one was open for 0% of the time, Pallas kernels for 0%

commit v1 on v0

--- a/solution.py
+++ b/solution.py
@@ -35,7 +35,7 @@
     return rounded.astype(jnp.float32)
 
 
-def body(tokens, routes, combine, prune_mask, gate_weight, up_weight, down_weight):
+def slotted_body(tokens, routes, combine, prune_mask, gate_weight, up_weight, down_weight):
     tok_dev, model_width = tokens.shape
     group_rows, top_k = routes.shape
     experts = lax.axis_size("expert")
@@ -61,6 +61,59 @@
     return mixed_out.astype(jnp.bfloat16)
 
 
+def exact_parts(values):
+    high = values.astype(jnp.bfloat16)
+    rest = values - high.astype(jnp.float32)
+    middle = rest.astype(jnp.bfloat16)
+    low = (rest - middle.astype(jnp.float32)).astype(jnp.bfloat16)
+    return high, middle, low
+
+
+def swap(block, distance, experts):
+    return lax.ppermute(block, "expert", [(i, i ^ distance) for i in range(experts)])
+
+
+def dense_body(tokens, routes, combine, prune_mask, gate_weight, up_weight, down_weight):
+    tok_dev, model_width = tokens.shape
+    experts = lax.axis_size("expert")
+    me = lax.axis_index("expert")
+    chosen = routes[:, :, None] == jnp.arange(experts, dtype=jnp.int32)[None, None, :]
+    shares = jnp.sum(jnp.where(chosen, combine[:, :, None], 0.0), axis=1)
+    extra = jnp.concatenate(exact_parts(shares), axis=1)
+    extra = jnp.pad(extra, ((0, 0), (0, -extra.shape[1] % 128)))
+    rows = jnp.concatenate([tokens, extra], axis=1)
+    distances = [1 << bit for bit in range(experts.bit_length() - 1)]
+    for distance in reversed(distances):
+        rows = jnp.concatenate([rows, swap(rows, distance, experts)], axis=0)
+    lane = jnp.arange(extra.shape[1], dtype=jnp.int32)[None, :]
+    mine = (lane % experts == me) & (lane < 3 * experts)
+    share = jnp.sum(jnp.where(mine, rows[:, model_width:].astype(jnp.float32), 0.0), axis=1)
+    keep_cols = jnp.repeat(prune_mask[0].astype(jnp.float32), BLK)
+    row_block = rows[:, :model_width]
+    gate_act = jnp.dot(row_block, gate_weight[0], preferred_element_type=jnp.float32)
+    up_act = jnp.dot(row_block, up_weight[0], preferred_element_type=jnp.float32)
+    hidden = (jax.nn.silu(gate_act) * up_act * keep_cols).astype(jnp.bfloat16)
+    answers = jnp.dot(hidden, down_weight[0], preferred_element_type=jnp.float32)
+    sums = (answers * share[:, None]).astype(jnp.bfloat16)
+    for distance in distances:
+        half = sums.shape[0] // 2
+        arrived = swap(sums[half:], distance, experts)
+        sums = (sums[:half].astype(jnp.float32) + arrived.astype(jnp.float32)).astype(jnp.bfloat16)
+    return sums
+
+
+def body(tokens, routes, combine, prune_mask, gate_weight, up_weight, down_weight):
+    experts = lax.axis_size("expert")
+    group_rows, top_k = routes.shape
+    full = 2 * group_rows * top_k // experts >= group_rows
+    paired = experts & (experts - 1) == 0
+    if full and paired and lax.axis_size("tensor") == 1:
+        chosen_body = dense_body
+    else:
+        chosen_body = slotted_body
+    return chosen_body(tokens, routes, combine, prune_mask, gate_weight, up_weight, down_weight)
+
+
 def solution(mesh):
     in_specs = (
         P(("groups", "expert", "tensor"), None),

time: 59.1 us -> 50.1 us (0.85)
  waiting for transfers between devices: 28.9 us -> 17.5 us
  other arithmetic: 3.07 us -> 7.94 us
  local copies, waits for them, and re-layouts: 7.69 us -> 3.69 us
  starting transfers between devices: 11.8 us -> 13.6 us
    all_to_all x2 -> x0, waiting for transfers between devices: 28.9 us -> none  [the longest x1 14.5 us: body(): lax.all_to_all(answers, 'expert', split_axis=0, concat_axis=0, tiled=True)]
    ppermute x0 -> x8, waiting for transfers between devices: none -> 17.5 us  [swap(): lax.ppermute(block, 'expert', [(i, i ^ distance) for i in range(experts)])]
    ppermute x0 -> x8, starting transfers between devices: none -> 13.6 us  [swap(): lax.ppermute(block, 'expert', [(i, i ^ distance) for i in range(experts)])]
    all_to_all x2 -> x0, starting transfers between devices: 11.8 us -> none  [the longest x1 7.41 us: body(): lax.all_to_all(outgoing, 'expert', split_axis=0, concat_axis=0, tiled=True)]
    gather x2 -> x0, local copies, waits for them, and re-layouts: 5.1 us -> none  [the longest x1 3 us: fill_slots(): outgoing = row_source[jnp.maximum(owners, 0)]]
    concatenate x0 -> x5, other arithmetic: none -> 3.77 us  [the longest x3 2.32 us: dense_body(): rows = jnp.concatenate([rows, swap(rows, distance, experts)], axis=0)]
    convert_element_type x2 -> x6, other arithmetic: 0.08 us -> 2.36 us  [the longest x4 1.7 us: dense_body(): (sums[:half].astype(jnp.float32) + arrived.astype(jnp.float32)).astype(jn...]
    select_n x3 -> x0, other arithmetic: 1.97 us -> none  [the longest x1 1.96 us: fill_slots(): outgoing = jnp.where(filled[:, None], outgoing, jnp.zeros_like(outgoing))]
  transfers between devices with their start and end apart: 2 -> 8, of which waited for: 2 -> 8; matrix products, arithmetic and copies ran while one was open for 0% -> 5% of each run, Pallas kernels for 0% -> 0%
where the time goes in v1:
time: 50.1 us; the launch traced here: 49.7 us
  waiting for transfers between devices  17.5 us (35%)
  starting transfers between devices  13.6 us (27%)
  other arithmetic  7.94 us (16%)
  matrix products  6.79 us (14%)
  local copies, waits for them, and re-layouts  3.69 us (7%)
    ppermute x8, waiting for transfers between devices, swap(): lax.ppermute(block, 'expert', [(i, i ^ distance) for i in range(experts)])  17.5 us
    ppermute x8, starting transfers between devices, swap(): lax.ppermute(block, 'expert', [(i, i ^ distance) for i in range(experts)])  13.6 us
    dot_general x1, matrix products, dense_body(): jnp.dot(hidden, down_weight[0], preferred_element_type=jnp.float32)  4.15 us
    dot_general x1, matrix products, dense_body(): jnp.dot(row_block, up_weight[0], preferred_element_type=jnp.float32)  2.65 us
    concatenate x3, other arithmetic, dense_body(): rows = jnp.concatenate([rows, swap(rows, distance, experts)], axis=0)  2.32 us
    unnamed x5, local copies, waits for them, and re-layouts  1.91 us
    convert_element_type x4, other arithmetic, dense_body(): (sums[:half].astype(jnp.float32) + arrived.astype(jnp.float32)).astype(jn...  1.7 us
    concatenate x1, other arithmetic, dense_body(): rows = jnp.concatenate([tokens, extra], axis=1)  1.38 us
  transfers between devices with their start and end apart: 8, of which 8 were waited for; matrix products, arithmetic and copies ran while one was open for 5% of the time, Pallas kernels for 0%

profile of v1, /device:TPU:0, one launch (start us, length us, event | category | flops | bytes accessed | tf_op | source)
XLA Modules:
  0.0 49.7 jit_solution(12619635285900822767)
XLA Ops:
  0.0 0.0 copy-start
  0.0 0.9 %select_reduce_fusion.1 = f32[8,16]{1,0:T(8,128)S(1)} fusion(f32[8,8]{1,0:T(8,128)} %param.9, s32[8,8]{1,0:T(8,128)} %param.8), kind=kLoop, calls=%fused_computation.22 | loop fusion | flops 2944 | bytes 1024 | tf_op jit(solution)/shard_map/reduce_sum | solution.py:81
  1.0 0.1 fusion.29
  1.0 1.4 %pad_maximum_fusion.3 = (bf16[8,2176]{1,0:T(8,128)(2,1)S(1)}, bf16[128,2176]{1,0:T(8,128)(2,1)}) fusion(bf16[8,128]{1,0:T(8,128)(2,1)S(1)} %fusion.29, bf16[8,2048]{1,0:T(8,128)(2,1)} %param.7), kind=kLoop, calls=%fused_computation.21 | loop fusion | flops 69631 | bytes 104448 | tf_op jit(solution)/shard_map/concatenate | solution.py:84
  2.4 4.0 %collective-permute-start = (bf16[8,2176]{1,0:T(8,128)(2,1)S(1)}, bf16[8,2176]{1,0:T(8,128)(2,1)S(1)}, u32[]{:S(2)}, u32[]{:S(2)}) collective-permute-start(bf16[8,2176]{1,0:T(8,128)(2,1)S(1)} %get-tuple-element.5), channel_id=1, source_target_pairs={{0,8},{1,9},{2,10},{3,11},{4,12},{5,13},{6,14},{7,15},{8,0},{9,1},... | collective-permute-start | bytes 104456 | tf_op jit(solution)/shard_map/ppermute | solution.py:73
  6.5 0.7 %convert_bitcast_fusion = f32[6]{0:T(128)S(1)} fusion(s32[1,6]{1,0:T(1,128)} %param.10), kind=kLoop, calls=%fused_computation.41 | loop fusion | flops 6 | bytes 48 | tf_op jit(solution)/shard_map/convert_element_type | solution.py:91
  7.1 0.1 broadcast_bitcast_fusion
  7.2 1.5 %collective-permute-done = bf16[8,2176]{1,0:T(8,128)(2,1)S(1)} collective-permute-done((bf16[8,2176]{1,0:T(8,128)(2,1)S(1)}, bf16[8,2176]{1,0:T(8,128)(2,1)S(1)}, u32[]{:S(2)}, u32[]{:S(2)}) %collective-permute-start) | collective-permute-done | bytes 34848 | tf_op jit(solution)/shard_map/ppermute | solution.py:73
  8.7 0.8 %pad_maximum_fusion.2 = bf16[16,2176]{1,0:T(8,128)(2,1)S(1)} fusion(bf16[8,2176]{1,0:T(8,128)(2,1)S(1)} %collective-permute-done, bf16[8,128]{1,0:T(8,128)(2,1)S(1)} %fusion.29, bf16[8,2048]{1,0:T(8,128)(2,1)} %param.7), kind=kLoop, calls=%fused_computation.18 | loop fusion | flops 208896 | bytes 139264 | tf_op jit(solution)/shard_map/concatenate | solution.py:87
  9.5 1.5 %collective-permute-start.1 = (bf16[16,2176]{1,0:T(8,128)(2,1)S(1)}, bf16[16,2176]{1,0:T(8,128)(2,1)S(1)}, u32[]{:S(2)}, u32[]{:S(2)}) collective-permute-start(bf16[16,2176]{1,0:T(8,128)(2,1)S(1)} %pad_maximum_fusion.2), channel_id=1, source_target_pairs={{0,4},{1,5},{2,6},{3,7},{4,0},{5,1},{6,2},{7,3},{8,12},{9,13},{10,... | collective-permute-start | bytes 208904 | tf_op jit(solution)/shard_map/ppermute | solution.py:73
  11.0 0.6 %constant_dynamic-update-slice_fusion.3 = bf16[128,2176]{1,0:T(8,128)(2,1)} fusion(bf16[128,2176]{1,0:T(8,128)(2,1)} %get-tuple-element.6, bf16[8,2176]{1,0:T(8,128)(2,1)S(1)} %collective-permute-done), kind=kLoop, calls=%fused_computation.27 | loop fusion | bytes 69632
  11.6 2.2 %collective-permute-done.1 = bf16[16,2176]{1,0:T(8,128)(2,1)S(1)} collective-permute-done((bf16[16,2176]{1,0:T(8,128)(2,1)S(1)}, bf16[16,2176]{1,0:T(8,128)(2,1)S(1)}, u32[]{:S(2)}, u32[]{:S(2)}) %collective-permute-start.1) | collective-permute-done | bytes 69664 | tf_op jit(solution)/shard_map/ppermute | solution.py:73
  13.8 0.8 %pad_maximum_fusion.1 = bf16[32,2176]{1,0:T(8,128)(2,1)S(1)} fusion(bf16[16,2176]{1,0:T(8,128)(2,1)S(1)} %collective-permute-done.1, bf16[8,2176]{1,0:T(8,128)(2,1)S(1)} %collective-permute-done, bf16[8,128]{1,0:T(8,128)(2,1)S(1)} %fusion.29, bf16[8,2048]{1,0:T(8,128)(2,1)} %param.7), kind=kLoop, calls=%fused_computation.16 | loop fusion | flops 557056 | bytes 278528 | tf_op jit(solution)/shard_map/concatenate | solution.py:87
  14.6 1.8 %collective-permute-start.2 = (bf16[32,2176]{1,0:T(8,128)(2,1)S(1)}, bf16[32,2176]{1,0:T(8,128)(2,1)S(1)}, u32[]{:S(2)}, u32[]{:S(2)}) collective-permute-start(bf16[32,2176]{1,0:T(8,128)(2,1)S(1)} %pad_maximum_fusion.1), channel_id=1, source_target_pairs={{0,2},{1,3},{2,0},{3,1},{4,6},{5,7},{6,4},{7,5},{8,10},{9,11},{10,... | collective-permute-start | bytes 417800 | tf_op jit(solution)/shard_map/ppermute | solution.py:73
  16.4 0.6 %constant_dynamic-update-slice_fusion.2 = bf16[128,2176]{1,0:T(8,128)(2,1)} fusion(bf16[128,2176]{1,0:T(8,128)(2,1)} %constant_dynamic-update-slice_fusion.3, bf16[16,2176]{1,0:T(8,128)(2,1)S(1)} %collective-permute-done.1), kind=kLoop, calls=%fused_computation.26 | loop fusion | bytes 139264
  17.0 2.7 %collective-permute-done.2 = bf16[32,2176]{1,0:T(8,128)(2,1)S(1)} collective-permute-done((bf16[32,2176]{1,0:T(8,128)(2,1)S(1)}, bf16[32,2176]{1,0:T(8,128)(2,1)S(1)}, u32[]{:S(2)}, u32[]{:S(2)}) %collective-permute-start.2) | collective-permute-done | bytes 139296 | tf_op jit(solution)/shard_map/ppermute | solution.py:73
  19.7 0.8 %pad_maximum_fusion = bf16[64,2176]{1,0:T(8,128)(2,1)S(1)} fusion(bf16[32,2176]{1,0:T(8,128)(2,1)S(1)} %collective-permute-done.2, bf16[16,2176]{1,0:T(8,128)(2,1)S(1)} %collective-permute-done.1, bf16[8,2176]{1,0:T(8,128)(2,1)S(1)} %collective-permute-done, bf16[8,128]{1,0:T(8,128)(2,1)S(1)} %fusion.29, bf16[8,2048]{1,0:T(8,128)(2,1)} %param.7), kind=kLoop, calls=%fused_computation.12 | loop fusion | flops 1392640 | bytes 557056 | tf_op jit(solution)/shard_map/concatenate | solution.py:87
  20.5 0.1 collective-permute-start.3
  20.6 0.7 %constant_dynamic-update-slice_fusion.1 = bf16[128,2176]{1,0:T(8,128)(2,1)} fusion(bf16[128,2176]{1,0:T(8,128)(2,1)} %constant_dynamic-update-slice_fusion.2, bf16[32,2176]{1,0:T(8,128)(2,1)S(1)} %collective-permute-done.2), kind=kLoop, calls=%fused_computation.25 | loop fusion | bytes 278528
  21.2 0.9 %collective-permute-done.3 = bf16[64,2176]{1,0:T(8,128)(2,1)S(1)} collective-permute-done((bf16[64,2176]{1,0:T(8,128)(2,1)S(1)}, bf16[64,2176]{1,0:T(8,128)(2,1)S(1)}, u32[]{:S(2)}, u32[]{:S(2)}) %collective-permute-start.3) | collective-permute-done | bytes 278560 | tf_op jit(solution)/shard_map/ppermute | solution.py:73
  22.1 0.7 %constant_dynamic-update-slice_fusion = bf16[128,2176]{1,0:T(8,128)(2,1)} fusion(bf16[128,2176]{1,0:T(8,128)(2,1)} %constant_dynamic-update-slice_fusion.1, bf16[64,2176]{1,0:T(8,128)(2,1)S(1)} %collective-permute-done.3), kind=kLoop, calls=%fused_computation.24 | loop fusion | bytes 557056 | tf_op jit(solution)/shard_map/concatenate | solution.py:87
  22.8 0.9 %select_reduce_fusion = f32[128]{0:T(128)S(1)} fusion(bf16[128,2176]{1,0:T(8,128)(2,1)} %constant_dynamic-update-slice_fusion, pred[128]{0:T(512)(128)(4,1)S(1)} %compare_and_fusion), kind=kLoop, calls=%fused_computation.20 | loop fusion | flops 49024 | bytes 33408 | tf_op jit(solution)/shard_map/reduce_sum | solution.py:90
  23.7 2.6 %fusion.2 = f32[128,768]{1,0:T(8,128)S(1)} fusion(bf16[1,2048,768]{2,1,0:T(8,128)(2,1)} %param.12, bf16[128,2176]{1,0:T(8,128)(2,1)} %constant_dynamic-update-slice_fusion), kind=kOutput, calls=%fused_computation.2 | convolution fusion | flops 402653184 | bytes 4063232 | tf_op jit(solution)/shard_map/dot_general | solution.py:94
  26.4 0.0 copy-done
  26.4 4.1 %fusion.9 = bf16[128,2048]{1,0:T(8,128)(2,1)} fusion(bf16[1,768,2048]{2,1,0:T(8,128)(2,1)S(1)} %copy-done, f32[128]{0:T(128)S(1)} %select_reduce_fusion, f32[128,768]{1,0:T(8,128)S(1)} %fusion.2, bf16[1,2048,768]{2,1,0:T(8,128)(2,1)} %param.11, bf16[128,2176]{1,0:T(8,128)(2,1)} %constant_dynamic-update-slice_fusion, f32[768]{0:T(1024)S(1)} %broadcast_bitcast_fusion), kind=kOutput, calls=%fused_computation.7 | convolution fusion | flops 806518784 | bytes 7736832 | tf_op jit(solution)/shard_map/dot_general | solution.py:96
  30.5 1.0 %slice.43 = bf16[64,2048]{1,0:T(8,128)(2,1)S(1)} slice(bf16[128,2048]{1,0:T(8,128)(2,1)} %fusion.9), slice={[64:128], [0:2048]} | slice | bytes 524288 | tf_op jit(solution)/shard_map/slice | solution.py:100
  31.5 0.2 collective-permute-start.4
  31.7 1.4 %collective-permute-done.4 = bf16[64,2048]{1,0:T(8,128)(2,1)S(1)} collective-permute-done((bf16[64,2048]{1,0:T(8,128)(2,1)S(1)}, bf16[64,2048]{1,0:T(8,128)(2,1)S(1)}, u32[]{:S(2)}, u32[]{:S(2)}) %collective-permute-start.4) | collective-permute-done | bytes 262176 | tf_op jit(solution)/shard_map/ppermute | solution.py:73
  33.1 1.0 %add_convert_fusion = bf16[64,2048]{1,0:T(8,128)(2,1)S(1)} fusion(bf16[64,2048]{1,0:T(8,128)(2,1)S(1)} %collective-permute-done.4, bf16[128,2048]{1,0:T(8,128)(2,1)} %fusion.9), kind=kLoop, calls=%fused_computation.8 | loop fusion | flops 524288 | bytes 786432 | tf_op jit(solution)/shard_map/convert_element_type | solution.py:101
  34.1 1.8 %collective-permute-start.5 = (bf16[32,2048]{1,0:T(8,128)(2,1)S(1)}, bf16[32,2048]{1,0:T(8,128)(2,1)S(1)}, u32[]{:S(2)}, u32[]{:S(2)}) collective-permute-start(bf16[32,2048]{1,0:T(8,128)(2,1)S(1)} %slice.45), channel_id=1, source_target_pairs={{0,2},{1,3},{2,0},{3,1},{4,6},{5,7},{6,4},{7,5},{8,10},{9,11},{10,... | collective-permute-start | bytes 393224 | tf_op jit(solution)/shard_map/ppermute | solution.py:73
  35.9 3.8 %collective-permute-done.5 = bf16[32,2048]{1,0:T(8,128)(2,1)S(1)} collective-permute-done((bf16[32,2048]{1,0:T(8,128)(2,1)S(1)}, bf16[32,2048]{1,0:T(8,128)(2,1)S(1)}, u32[]{:S(2)}, u32[]{:S(2)}) %collective-permute-start.5) | collective-permute-done | bytes 131104 | tf_op jit(solution)/shard_map/ppermute | solution.py:73
  39.8 1.6 %collective-permute-start.6 = (bf16[16,2048]{1,0:T(8,128)(2,1)S(1)}, bf16[16,2048]{1,0:T(8,128)(2,1)S(1)}, u32[]{:S(2)}, u32[]{:S(2)}) collective-permute-start(bf16[16,2048]{1,0:T(8,128)(2,1)S(1)} %slice.47), channel_id=1, source_target_pairs={{0,4},{1,5},{2,6},{3,7},{4,0},{5,1},{6,2},{7,3},{8,12},{9,13},{10,... | collective-permute-start | bytes 196616 | tf_op jit(solution)/shard_map/ppermute | solution.py:73
  41.4 2.7 %collective-permute-done.6 = bf16[16,2048]{1,0:T(8,128)(2,1)S(1)} collective-permute-done((bf16[16,2048]{1,0:T(8,128)(2,1)S(1)}, bf16[16,2048]{1,0:T(8,128)(2,1)S(1)}, u32[]{:S(2)}, u32[]{:S(2)}) %collective-permute-start.6) | collective-permute-done | bytes 65568 | tf_op jit(solution)/shard_map/ppermute | solution.py:73
  44.2 2.6 %collective-permute-start.7 = (bf16[8,2048]{1,0:T(8,128)(2,1)S(1)}, bf16[8,2048]{1,0:T(8,128)(2,1)S(1)}, u32[]{:S(2)}, u32[]{:S(2)}) collective-permute-start(bf16[8,2048]{1,0:T(8,128)(2,1)S(1)} %slice.49), channel_id=1, source_target_pairs={{0,8},{1,9},{2,10},{3,11},{4,12},{5,13},{6,14},{7,15},{8,0},{9,1},... | collective-permute-start | bytes 98312 | tf_op jit(solution)/shard_map/ppermute | solution.py:73
  46.8 2.2 %collective-permute-done.7 = bf16[8,2048]{1,0:T(8,128)(2,1)S(1)} collective-permute-done((bf16[8,2048]{1,0:T(8,128)(2,1)S(1)}, bf16[8,2048]{1,0:T(8,128)(2,1)S(1)}, u32[]{:S(2)}, u32[]{:S(2)}) %collective-permute-start.7) | collective-permute-done | bytes 32800 | tf_op jit(solution)/shard_map/ppermute | solution.py:73
  49.0 0.6 %add_convert_fusion.3 = bf16[8,2048]{1,0:T(8,128)(2,1)} fusion(bf16[8,2048]{1,0:T(8,128)(2,1)S(1)} %collective-permute-done.7, bf16[16,2048]{1,0:T(8,128)(2,1)S(1)} %add_convert_fusion.2), kind=kLoop, calls=%fused_computation.19 | loop fusion | flops 65536 | bytes 98304 | tf_op jit(solution)/shard_map/convert_element_type | solution.py:101
  (7 shorter events, 0.1 us)
Async XLA Ops:
  0.0 26.4 %copy-start = (bf16[1,768,2048]{2,1,0:T(8,128)(2,1)S(1)}, bf16[1,768,2048]{2,1,0:T(8,128)(2,1)}, u32[]{:S(2)}) copy-start(bf16[1,768,2048]{2,1,0:T(8,128)(2,1)} %param.13) | copy-start | bytes 9437188
  2.4 6.3 %collective-permute-start = (bf16[8,2176]{1,0:T(8,128)(2,1)S(1)}, bf16[8,2176]{1,0:T(8,128)(2,1)S(1)}, u32[]{:S(2)}, u32[]{:S(2)}) collective-permute-start(bf16[8,2176]{1,0:T(8,128)(2,1)S(1)} %get-tuple-element.5), channel_id=1, source_target_pairs={{0,8},{1,9},{2,10},{3,11},{4,12},{5,13},{6,14},{7,15},{8,0},{9,1},... | collective-permute-start | bytes 104456 | tf_op jit(solution)/shard_map/ppermute | solution.py:73
  9.5 4.3 %collective-permute-start.1 = (bf16[16,2176]{1,0:T(8,128)(2,1)S(1)}, bf16[16,2176]{1,0:T(8,128)(2,1)S(1)}, u32[]{:S(2)}, u32[]{:S(2)}) collective-permute-start(bf16[16,2176]{1,0:T(8,128)(2,1)S(1)} %pad_maximum_fusion.2), channel_id=1, source_target_pairs={{0,4},{1,5},{2,6},{3,7},{4,0},{5,1},{6,2},{7,3},{8,12},{9,13},{10,... | collective-permute-start | bytes 208904 | tf_op jit(solution)/shard_map/ppermute | solution.py:73
  14.6 5.1 %collective-permute-start.2 = (bf16[32,2176]{1,0:T(8,128)(2,1)S(1)}, bf16[32,2176]{1,0:T(8,128)(2,1)S(1)}, u32[]{:S(2)}, u32[]{:S(2)}) collective-permute-start(bf16[32,2176]{1,0:T(8,128)(2,1)S(1)} %pad_maximum_fusion.1), channel_id=1, source_target_pairs={{0,2},{1,3},{2,0},{3,1},{4,6},{5,7},{6,4},{7,5},{8,10},{9,11},{10,... | collective-permute-start | bytes 417800 | tf_op jit(solution)/shard_map/ppermute | solution.py:73
  20.5 1.6 %collective-permute-start.3 = (bf16[64,2176]{1,0:T(8,128)(2,1)S(1)}, bf16[64,2176]{1,0:T(8,128)(2,1)S(1)}, u32[]{:S(2)}, u32[]{:S(2)}) collective-permute-start(bf16[64,2176]{1,0:T(8,128)(2,1)S(1)} %pad_maximum_fusion), channel_id=1, source_target_pairs={{0,1},{1,0},{2,3},{3,2},{4,5},{5,4},{6,7},{7,6},{8,9},{9,8},{10,11... | collective-permute-start | bytes 835592 | tf_op jit(solution)/shard_map/ppermute | solution.py:73
  31.5 1.6 %collective-permute-start.4 = (bf16[64,2048]{1,0:T(8,128)(2,1)S(1)}, bf16[64,2048]{1,0:T(8,128)(2,1)S(1)}, u32[]{:S(2)}, u32[]{:S(2)}) collective-permute-start(bf16[64,2048]{1,0:T(8,128)(2,1)S(1)} %slice.43), channel_id=1, source_target_pairs={{0,1},{1,0},{2,3},{3,2},{4,5},{5,4},{6,7},{7,6},{8,9},{9,8},{10,11... | collective-permute-start | bytes 786440 | tf_op jit(solution)/shard_map/ppermute | solution.py:73
  34.1 5.6 %collective-permute-start.5 = (bf16[32,2048]{1,0:T(8,128)(2,1)S(1)}, bf16[32,2048]{1,0:T(8,128)(2,1)S(1)}, u32[]{:S(2)}, u32[]{:S(2)}) collective-permute-start(bf16[32,2048]{1,0:T(8,128)(2,1)S(1)} %slice.45), channel_id=1, source_target_pairs={{0,2},{1,3},{2,0},{3,1},{4,6},{5,7},{6,4},{7,5},{8,10},{9,11},{10,... | collective-permute-start | bytes 393224 | tf_op jit(solution)/shard_map/ppermute | solution.py:73
  39.8 4.3 %collective-permute-start.6 = (bf16[16,2048]{1,0:T(8,128)(2,1)S(1)}, bf16[16,2048]{1,0:T(8,128)(2,1)S(1)}, u32[]{:S(2)}, u32[]{:S(2)}) collective-permute-start(bf16[16,2048]{1,0:T(8,128)(2,1)S(1)} %slice.47), channel_id=1, source_target_pairs={{0,4},{1,5},{2,6},{3,7},{4,0},{5,1},{6,2},{7,3},{8,12},{9,13},{10,... | collective-permute-start | bytes 196616 | tf_op jit(solution)/shard_map/ppermute | solution.py:73
  44.2 4.9 %collective-permute-start.7 = (bf16[8,2048]{1,0:T(8,128)(2,1)S(1)}, bf16[8,2048]{1,0:T(8,128)(2,1)S(1)}, u32[]{:S(2)}, u32[]{:S(2)}) collective-permute-start(bf16[8,2048]{1,0:T(8,128)(2,1)S(1)} %slice.49), channel_id=1, source_target_pairs={{0,8},{1,9},{2,10},{3,11},{4,12},{5,13},{6,14},{7,15},{8,0},{9,1},... | collective-permute-start | bytes 98312 | tf_op jit(solution)/shard_map/ppermute | solution.py:73

commit v2 on v0

--- a/solution.py
+++ b/solution.py
@@ -1,6 +1,10 @@
+import functools
+
 import jax
 import jax.numpy as jnp
 from jax import lax
+from jax.experimental import pallas as pl
+from jax.experimental.pallas import tpu as pltpu
 from jax.sharding import PartitionSpec as P
 
 BLK = 128
@@ -35,7 +39,7 @@
     return rounded.astype(jnp.float32)
 
 
-def body(tokens, routes, combine, prune_mask, gate_weight, up_weight, down_weight):
+def slotted_body(tokens, routes, combine, prune_mask, gate_weight, up_weight, down_weight):
     tok_dev, model_width = tokens.shape
     group_rows, top_k = routes.shape
     experts = lax.axis_size("expert")
@@ -61,6 +65,147 @@
     return mixed_out.astype(jnp.bfloat16)
 
 
+WHOLE = pl.BlockSpec(memory_space=pltpu.VMEM)
+ANYWHERE = pl.BlockSpec(memory_space=pl.ANY)
+
+
+def swap(block, distance, experts):
+    return lax.ppermute(block, "expert", [(i, i ^ distance) for i in range(experts)])
+
+
+def joined(*blocks):
+    return lax.optimization_barrier(jnp.concatenate(blocks, axis=0))
+
+
+def add(a, b):
+    return (a.astype(jnp.float32) + b.astype(jnp.float32)).astype(jnp.bfloat16)
+
+
+def pack_kernel(tokens_ref, share_ref, out_ref):
+    width = tokens_ref.shape[1]
+    share = share_ref[...]
+    experts = share.shape[1] // 3
+    high = share.astype(jnp.bfloat16).astype(jnp.float32)
+    middle = (share - high).astype(jnp.bfloat16).astype(jnp.float32)
+    low = share - high - middle
+    part = lax.broadcasted_iota(jnp.int32, share.shape, 1) // experts
+    extra = jnp.where(part == 0, high, jnp.where(part == 1, middle, low))
+    out_ref[:, :width] = tokens_ref[...]
+    out_ref[:, width:] = jnp.zeros((tokens_ref.shape[0], out_ref.shape[1] - width), jnp.bfloat16)
+    out_ref[:, width : width + 3 * experts] = extra.astype(jnp.bfloat16)
+
+
+def load_kernel(source, after, target, sems):
+    del after
+    count = sems.shape[0]
+    rows = source.shape[1] // count
+    copies = [
+        pltpu.make_async_copy(source.at[:, i * rows : (i + 1) * rows], target.at[:, i * rows : (i + 1) * rows], sems.at[i])
+        for i in range(count)
+    ]
+    for copy in copies:
+        copy.start()
+    for copy in copies:
+        copy.wait()
+
+
+def load(source, after):
+    return pl.pallas_call(
+        load_kernel,
+        out_shape=jax.ShapeDtypeStruct(source.shape, source.dtype),
+        in_specs=[ANYWHERE] * 2,
+        out_specs=WHOLE,
+        scratch_shapes=[pltpu.SemaphoreType.DMA((4,))],
+        cost_estimate=pl.CostEstimate(flops=0, bytes_accessed=2 * source.size, transcendentals=0),
+        compiler_params=pltpu.CompilerParams(vmem_limit_bytes=1 << 20),
+    )(source, after)
+
+
+def expert_kernel(experts, n_pieces, *refs):
+    pieces = refs[:n_pieces]
+    mask_ref, gate_ref, up_ref, down_ref, keep_ref, send_ref, rows, hidden = refs[n_pieces:]
+    width, units = gate_ref.shape[1:]
+    me = lax.axis_index("expert")
+    spots = []
+    at = 0
+    for piece in pieces:
+        count = piece.shape[0]
+        rows[at : at + count, :] = piece[:, :width]
+        extra = piece[:, width:]
+        lane = lax.broadcasted_iota(jnp.int32, extra.shape, 1)
+        mine = (lane % experts == me) & (lane < 3 * experts)
+        spots.append(jnp.sum(jnp.where(mine, extra.astype(jnp.float32), 0.0), axis=1, keepdims=True))
+        at += count
+    share = jnp.concatenate(spots, axis=0)
+    for j in range(units // BLK):
+        cols = slice(j * BLK, (j + 1) * BLK)
+        keep = mask_ref[0, j].astype(jnp.float32)
+        gate_act = jnp.dot(rows[...], gate_ref[0, :, cols], preferred_element_type=jnp.float32)
+        up_act = jnp.dot(rows[...], up_ref[0, :, cols], preferred_element_type=jnp.float32)
+        value = gate_act / (1.0 + jnp.exp(-gate_act)) * up_act * keep
+        hidden[:, cols] = value.astype(jnp.bfloat16)
+    half = rows.shape[0] // 2
+    step = 512 if width % 512 == 0 else BLK
+    for j in range(width // step):
+        cols = slice(j * step, (j + 1) * step)
+        answer = jnp.dot(hidden[...], down_ref[0, :, cols], preferred_element_type=jnp.float32)
+        answer = (answer * share).astype(jnp.bfloat16)
+        keep_ref[:, cols] = answer[:half]
+        send_ref[:, cols] = answer[half:]
+
+
+def dense_body(tokens, routes, combine, prune_mask, gate_weight, up_weight, down_weight):
+    tok_dev, model_width = tokens.shape
+    units = gate_weight.shape[2]
+    experts = lax.axis_size("expert")
+    distances = [1 << bit for bit in range(experts.bit_length() - 1)]
+    lanes = jnp.arange(3 * experts, dtype=jnp.int32) % experts
+    chosen = routes[:, :, None] == lanes[None, None, :]
+    shares = jnp.sum(jnp.where(chosen, combine[:, :, None], 0.0), axis=1)
+    rows = pl.pallas_call(
+        pack_kernel,
+        out_shape=jax.ShapeDtypeStruct((tok_dev, model_width + BLK), jnp.bfloat16),
+        in_specs=[WHOLE] * 2,
+        out_specs=WHOLE,
+        compiler_params=pltpu.CompilerParams(vmem_limit_bytes=1 << 20),
+    )(tokens, shares)
+    weights = []
+    for distance, weight in zip(reversed(distances[1:]), (gate_weight, up_weight, down_weight)):
+        loaded = load(weight, rows)
+        both = jnp.concatenate([rows, swap(rows, distance, experts)], axis=0)
+        rows, loaded = lax.optimization_barrier((both, loaded))
+        weights.append(loaded)
+    pieces = [rows, swap(rows, distances[0], experts)]
+    total = sum(piece.shape[0] for piece in pieces)
+    out = jax.ShapeDtypeStruct((total // 2, model_width), jnp.bfloat16)
+    kept, sent = pl.pallas_call(
+        functools.partial(expert_kernel, experts, len(pieces)),
+        out_shape=(out, out),
+        in_specs=[WHOLE] * len(pieces) + [pl.BlockSpec(memory_space=pltpu.SMEM)] + [WHOLE] * 3,
+        out_specs=(WHOLE, WHOLE),
+        scratch_shapes=[pltpu.VMEM((total, model_width), jnp.bfloat16), pltpu.VMEM((total, units), jnp.bfloat16)],
+        compiler_params=pltpu.CompilerParams(vmem_limit_bytes=16 << 20),
+    )(*pieces, prune_mask, *weights)
+    arrived = swap(sent, distances[0], experts)
+    for distance in distances[1:]:
+        half = kept.shape[0] // 2
+        sent = lax.optimization_barrier(add(kept[half:], arrived[half:]))
+        kept = add(kept[:half], arrived[:half])
+        arrived = swap(sent, distance, experts)
+    return add(kept, arrived)
+
+
+def body(tokens, routes, combine, prune_mask, gate_weight, up_weight, down_weight):
+    experts = lax.axis_size("expert")
+    group_rows, top_k = routes.shape
+    full = 2 * group_rows * top_k // experts >= group_rows
+    if full and experts == 16 and lax.axis_size("tensor") == 1:
+        chosen_body = dense_body
+    else:
+        chosen_body = slotted_body
+    return chosen_body(tokens, routes, combine, prune_mask, gate_weight, up_weight, down_weight)
+
+
 def solution(mesh):
     in_specs = (
         P(("groups", "expert", "tensor"), None),

time: 59.1 us -> 39.4 us (0.67)
  waiting for transfers between devices: 28.9 us -> 17.5 us
  matrix products: 6.98 us -> 0 us
  local copies, waits for them, and re-layouts: 7.69 us -> 2.66 us
  Pallas kernels: 0 us -> 3.63 us
  starting transfers between devices: 11.8 us -> 13.7 us
  other arithmetic: 3.07 us -> 1.58 us
    all_to_all x2 -> x0, waiting for transfers between devices: 28.9 us -> none  [the longest x1 14.5 us: body(): lax.all_to_all(answers, 'expert', split_axis=0, concat_axis=0, tiled=True)]
    ppermute x0 -> x8, waiting for transfers between devices: none -> 17.5 us  [swap(): lax.ppermute(block, 'expert', [(i, i ^ distance) for i in range(experts)])]
    ppermute x0 -> x8, starting transfers between devices: none -> 13.7 us  [swap(): lax.ppermute(block, 'expert', [(i, i ^ distance) for i in range(experts)])]
    all_to_all x2 -> x0, starting transfers between devices: 11.8 us -> none  [the longest x1 7.41 us: body(): lax.all_to_all(outgoing, 'expert', split_axis=0, concat_axis=0, tiled=True)]
    dot_general x3 -> x0, matrix products: 6.98 us -> none  [the longest x1 4.14 us: expert_partial(): jnp.dot(hidden, down_weight[0], preferred_element_type=jnp.float32)]
    gather x2 -> x0, local copies, waits for them, and re-layouts: 5.1 us -> none  [the longest x1 3 us: fill_slots(): outgoing = row_source[jnp.maximum(owners, 0)]]
    pallas_call x0 -> x5, Pallas kernels: none -> 3.63 us  [the longest x1 2.86 us: dense_body(): pl.pallas_call(functools.partial(expert_kernel, experts, len(pieces)), ou...]
    unnamed x6 -> x10, local copies, waits for them, and re-layouts: 0.01 us -> 2.66 us
  transfers between devices with their start and end apart: 2 -> 8, of which waited for: 2 -> 8; matrix products, arithmetic and copies ran while one was open for 0% -> 0% of each run, Pallas kernels for 0% -> 2%
where the time goes in v2:
time: 39.4 us; the launch traced here: 39.2 us
  waiting for transfers between devices  17.5 us (44%)
  starting transfers between devices  13.7 us (35%)
  Pallas kernels  3.63 us (9%)
  local copies, waits for them, and re-layouts  2.66 us (7%)
  other arithmetic  1.58 us (4%)
    ppermute x8, waiting for transfers between devices, swap(): lax.ppermute(block, 'expert', [(i, i ^ distance) for i in range(experts)])  17.5 us
    ppermute x8, starting transfers between devices, swap(): lax.ppermute(block, 'expert', [(i, i ^ distance) for i in range(experts)])  13.7 us
    pallas_call x1, Pallas kernels, dense_body(): pl.pallas_call(functools.partial(expert_kernel, experts, len(pieces)), ou...  2.86 us
    unnamed x10, local copies, waits for them, and re-layouts  2.66 us
    reduce_sum x1, other arithmetic, dense_body(): shares = jnp.sum(jnp.where(chosen, combine[:, :, None], 0.0), axis=1)  0.79 us
  transfers between devices with their start and end apart: 8, of which 8 were waited for; matrix products, arithmetic and copies ran while one was open for 0% of the time, Pallas kernels for 2%

profile of v2, /device:TPU:0, one launch (start us, length us, event | category | flops | bytes accessed | tf_op | source)
XLA Modules:
  0.0 39.2 jit_solution(15180083569509533339)
XLA Ops:
  0.0 0.8 %select_reduce_fusion.share_ref = f32[8,48]{1,0:T(8,128)S(1)} fusion(f32[8,8]{1,0:T(8,128)} %param.9, s32[48]{0:T(128)S(1)} %and_select_fusion, s32[8,8]{1,0:T(8,128)} %param.8), kind=kLoop, calls=%fused_computation.10 | loop fusion | flops 8832 | bytes 2240 | tf_op jit(solution)/shard_map/reduce_sum | solution.py:164
  0.8 0.0 copy-start.3
  0.8 0.7 %copy-done.3 = bf16[8,2048]{1,0:T(8,128)(2,1)S(1)} copy-done((bf16[8,2048]{1,0:T(8,128)(2,1)S(1)}, bf16[8,2048]{1,0:T(8,128)(2,1)}, u32[]{:S(2)}) %copy-start.3) | copy-done | bytes 32792
  1.6 4.1 %collective-permute-start = (bf16[8,2176]{1,0:T(8,128)(2,1)S(1)}, bf16[8,2176]{1,0:T(8,128)(2,1)S(1)}, u32[]{:S(2)}, u32[]{:S(2)}) collective-permute-start(bf16[8,2176]{1,0:T(8,128)(2,1)S(1)} %shard_map.73.after), channel_id=1, source_target_pairs={{0,8},{1,9},{2,10},{3,11},{4,12},{5,13},{6,14},{7,15},{8,0},{9,1},... | collective-permute-start | bytes 104456 | tf_op jit(solution)/shard_map/ppermute | solution.py:73
  5.7 0.0 copy-start
  5.7 1.9 %copy-done = bf16[1,2048,768]{2,1,0:T(8,128)(2,1)S(1)} copy-done((bf16[1,2048,768]{2,1,0:T(8,128)(2,1)S(1)}, bf16[1,2048,768]{2,1,0:T(8,128)(2,1)}, u32[]{:S(2)}) %copy-start) | copy-done | bytes 3145752
  7.6 0.0 copy-start.2
  7.6 0.3 shard_map.74.refs_3_
  7.8 0.1 collective-permute-done
  8.0 0.0 copy-start.1
  8.0 1.6 %collective-permute-start.1 = (bf16[16,2176]{1,0:T(8,128)(2,1)S(1)}, bf16[16,2176]{1,0:T(8,128)(2,1)S(1)}, u32[]{:S(2)}, u32[]{:S(2)}) collective-permute-start(bf16[16,2176]{1,0:T(8,128)(2,1)S(1)} %pad_maximum_fusion.2.after), channel_id=1, source_target_pairs={{0,4},{1,5},{2,6},{3,7},{4,0},{5,1},{6,2},{7,3},{8,12},{9,13},{10,... | collective-permute-start | bytes 208904 | tf_op jit(solution)/shard_map/ppermute | solution.py:73
  9.6 0.0 copy-done.2
  9.6 0.3 shard_map.75.refs_4_
  9.8 2.5 %collective-permute-done.1 = bf16[16,2176]{1,0:T(8,128)(2,1)S(1)} collective-permute-done((bf16[16,2176]{1,0:T(8,128)(2,1)S(1)}, bf16[16,2176]{1,0:T(8,128)(2,1)S(1)}, u32[]{:S(2)}, u32[]{:S(2)}) %collective-permute-start.1) | collective-permute-done | bytes 69664 | tf_op jit(solution)/shard_map/ppermute | solution.py:73
  12.4 0.0 copy-start.4
  12.4 1.8 %collective-permute-start.2 = (bf16[32,2176]{1,0:T(8,128)(2,1)S(1)}, bf16[32,2176]{1,0:T(8,128)(2,1)S(1)}, u32[]{:S(2)}, u32[]{:S(2)}) collective-permute-start(bf16[32,2176]{1,0:T(8,128)(2,1)S(1)} %pad_maximum_fusion.1.after), channel_id=1, source_target_pairs={{0,2},{1,3},{2,0},{3,1},{4,6},{5,7},{6,4},{7,5},{8,10},{9,11},{10,... | collective-permute-start | bytes 417800 | tf_op jit(solution)/shard_map/ppermute | solution.py:73
  14.1 0.0 copy-done.1
  14.1 0.3 shard_map.76.refs_5_
  14.4 3.1 %collective-permute-done.2 = bf16[32,2176]{1,0:T(8,128)(2,1)S(1)} collective-permute-done((bf16[32,2176]{1,0:T(8,128)(2,1)S(1)}, bf16[32,2176]{1,0:T(8,128)(2,1)S(1)}, u32[]{:S(2)}, u32[]{:S(2)}) %collective-permute-start.2) | collective-permute-done | bytes 139296 | tf_op jit(solution)/shard_map/ppermute | solution.py:73
  17.5 0.1 collective-permute-start.3
  17.6 1.5 %collective-permute-done.3.refs_1_ = bf16[64,2176]{1,0:T(8,128)(2,1)S(1)} collective-permute-done((bf16[64,2176]{1,0:T(8,128)(2,1)S(1)}, bf16[64,2176]{1,0:T(8,128)(2,1)S(1)}, u32[]{:S(2)}, u32[]{:S(2)}) %collective-permute-start.3) | collective-permute-done | bytes 278560 | tf_op jit(solution)/shard_map/ppermute | solution.py:73
  19.2 0.0 copy-done.4
  19.2 2.9 %shard_map.77 = (bf16[64,2048]{1,0:T(8,128)(2,1)S(1)}, bf16[64,2048]{1,0:T(8,128)(2,1)S(1)}) custom-call(bf16[64,2176]{1,0:T(8,128)(2,1)S(1)} %pad_maximum_fusion.refs_0_, bf16[64,2176]{1,0:T(8,128)(2,1)S(1)} %collective-permute-done.3.refs_1_, s32[1,6]{1,0:T(1,128)S(1)} %copy-done.4, bf16[1,2048,768]{2,1,0:T(8,128)(2,1)S(1)} %shard_map.74.refs_3_, ...), custom_call_target="tpu_custom_call" | custom-call | tf_op jit(solution)/shard_map/pallas_call | solution.py:181
  22.0 0.2 collective-permute-start.4
  22.2 1.4 %collective-permute-done.4 = bf16[64,2048]{1,0:T(8,128)(2,1)S(1)} collective-permute-done((bf16[64,2048]{1,0:T(8,128)(2,1)S(1)}, bf16[64,2048]{1,0:T(8,128)(2,1)S(1)}, u32[]{:S(2)}, u32[]{:S(2)}) %collective-permute-start.4) | collective-permute-done | bytes 262176 | tf_op jit(solution)/shard_map/ppermute | solution.py:73
  23.6 0.1 add_convert_fusion.1
  23.7 1.8 %collective-permute-start.5 = (bf16[32,2048]{1,0:T(8,128)(2,1)S(1)}, bf16[32,2048]{1,0:T(8,128)(2,1)S(1)}, u32[]{:S(2)}, u32[]{:S(2)}) collective-permute-start(bf16[32,2048]{1,0:T(8,128)(2,1)S(1)} %get-tuple-element.22), channel_id=1, source_target_pairs={{0,2},{1,3},{2,0},{3,1},{4,6},{5,7},{6,4},{7,5},{8,10},{9,11},{10,... | collective-permute-start | bytes 393224 | tf_op jit(solution)/shard_map/ppermute | solution.py:73
  25.5 3.9 %collective-permute-done.5 = bf16[32,2048]{1,0:T(8,128)(2,1)S(1)} collective-permute-done((bf16[32,2048]{1,0:T(8,128)(2,1)S(1)}, bf16[32,2048]{1,0:T(8,128)(2,1)S(1)}, u32[]{:S(2)}, u32[]{:S(2)}) %collective-permute-start.5) | collective-permute-done | bytes 131104 | tf_op jit(solution)/shard_map/ppermute | solution.py:73
  29.3 1.6 %collective-permute-start.6 = (bf16[16,2048]{1,0:T(8,128)(2,1)S(1)}, bf16[16,2048]{1,0:T(8,128)(2,1)S(1)}, u32[]{:S(2)}, u32[]{:S(2)}) collective-permute-start(bf16[16,2048]{1,0:T(8,128)(2,1)S(1)} %get-tuple-element.24), channel_id=1, source_target_pairs={{0,4},{1,5},{2,6},{3,7},{4,0},{5,1},{6,2},{7,3},{8,12},{9,13},{10,... | collective-permute-start | bytes 196616 | tf_op jit(solution)/shard_map/ppermute | solution.py:73
  30.9 2.7 %collective-permute-done.6 = bf16[16,2048]{1,0:T(8,128)(2,1)S(1)} collective-permute-done((bf16[16,2048]{1,0:T(8,128)(2,1)S(1)}, bf16[16,2048]{1,0:T(8,128)(2,1)S(1)}, u32[]{:S(2)}, u32[]{:S(2)}) %collective-permute-start.6) | collective-permute-done | bytes 65568 | tf_op jit(solution)/shard_map/ppermute | solution.py:73
  33.7 2.6 %collective-permute-start.7 = (bf16[8,2048]{1,0:T(8,128)(2,1)S(1)}, bf16[8,2048]{1,0:T(8,128)(2,1)S(1)}, u32[]{:S(2)}, u32[]{:S(2)}) collective-permute-start(bf16[8,2048]{1,0:T(8,128)(2,1)S(1)} %add_convert_fusion.5), channel_id=1, source_target_pairs={{0,8},{1,9},{2,10},{3,11},{4,12},{5,13},{6,14},{7,15},{8,0},{9,1},... | collective-permute-start | bytes 98312 | tf_op jit(solution)/shard_map/ppermute | solution.py:73
  36.3 2.2 %collective-permute-done.7 = bf16[8,2048]{1,0:T(8,128)(2,1)S(1)} collective-permute-done((bf16[8,2048]{1,0:T(8,128)(2,1)S(1)}, bf16[8,2048]{1,0:T(8,128)(2,1)S(1)}, u32[]{:S(2)}, u32[]{:S(2)}) %collective-permute-start.7) | collective-permute-done | bytes 32800 | tf_op jit(solution)/shard_map/ppermute | solution.py:73
  38.6 0.6 %add_convert_fusion.4 = bf16[8,2048]{1,0:T(8,128)(2,1)} fusion(bf16[8,2048]{1,0:T(8,128)(2,1)S(1)} %collective-permute-done.7, bf16[16,2048]{1,0:T(8,128)(2,1)S(1)} %collective-permute-done.6, bf16[16,2048]{1,0:T(8,128)(2,1)S(1)} %get-tuple-element.23), kind=kLoop, calls=%fused_computation.7 | loop fusion | flops 131072 | bytes 131072 | tf_op jit(solution)/shard_map/convert_element_type | solution.py:81
  (7 shorter events, 0.1 us)
Async XLA Ops:
  0.8 0.8 %copy-start.3 = (bf16[8,2048]{1,0:T(8,128)(2,1)S(1)}, bf16[8,2048]{1,0:T(8,128)(2,1)}, u32[]{:S(2)}) copy-start(bf16[8,2048]{1,0:T(8,128)(2,1)} %tokens_ref.1) | copy-start | bytes 98308
  1.6 6.4 %collective-permute-start = (bf16[8,2176]{1,0:T(8,128)(2,1)S(1)}, bf16[8,2176]{1,0:T(8,128)(2,1)S(1)}, u32[]{:S(2)}, u32[]{:S(2)}) collective-permute-start(bf16[8,2176]{1,0:T(8,128)(2,1)S(1)} %shard_map.73.after), channel_id=1, source_target_pairs={{0,8},{1,9},{2,10},{3,11},{4,12},{5,13},{6,14},{7,15},{8,0},{9,1},... | collective-permute-start | bytes 104456 | tf_op jit(solution)/shard_map/ppermute | solution.py:73
  5.7 1.9 %copy-start = (bf16[1,2048,768]{2,1,0:T(8,128)(2,1)S(1)}, bf16[1,2048,768]{2,1,0:T(8,128)(2,1)}, u32[]{:S(2)}) copy-start(bf16[1,2048,768]{2,1,0:T(8,128)(2,1)} %source.3) | copy-start | bytes 9437188
  7.6 2.0 %copy-start.2 = (bf16[1,2048,768]{2,1,0:T(8,128)(2,1)S(1)}, bf16[1,2048,768]{2,1,0:T(8,128)(2,1)}, u32[]{:S(2)}) copy-start(bf16[1,2048,768]{2,1,0:T(8,128)(2,1)} %source.4) | copy-start | bytes 9437188
  8.0 6.2 %copy-start.1 = (bf16[1,768,2048]{2,1,0:T(8,128)(2,1)S(1)}, bf16[1,768,2048]{2,1,0:T(8,128)(2,1)}, u32[]{:S(2)}) copy-start(bf16[1,768,2048]{2,1,0:T(8,128)(2,1)} %source.5) | copy-start | bytes 9437188
  8.0 4.4 %collective-permute-start.1 = (bf16[16,2176]{1,0:T(8,128)(2,1)S(1)}, bf16[16,2176]{1,0:T(8,128)(2,1)S(1)}, u32[]{:S(2)}, u32[]{:S(2)}) collective-permute-start(bf16[16,2176]{1,0:T(8,128)(2,1)S(1)} %pad_maximum_fusion.2.after), channel_id=1, source_target_pairs={{0,4},{1,5},{2,6},{3,7},{4,0},{5,1},{6,2},{7,3},{8,12},{9,13},{10,... | collective-permute-start | bytes 208904 | tf_op jit(solution)/shard_map/ppermute | solution.py:73
  12.4 6.8 %copy-start.4 = (s32[1,6]{1,0:T(1,128)S(1)}, s32[1,6]{1,0:T(1,128)}, u32[]{:S(2)}) copy-start(s32[1,6]{1,0:T(1,128)} %refs_2_.1) | copy-start | bytes 76
  12.4 5.1 %collective-permute-start.2 = (bf16[32,2176]{1,0:T(8,128)(2,1)S(1)}, bf16[32,2176]{1,0:T(8,128)(2,1)S(1)}, u32[]{:S(2)}, u32[]{:S(2)}) collective-permute-start(bf16[32,2176]{1,0:T(8,128)(2,1)S(1)} %pad_maximum_fusion.1.after), channel_id=1, source_target_pairs={{0,2},{1,3},{2,0},{3,1},{4,6},{5,7},{6,4},{7,5},{8,10},{9,11},{10,... | collective-permute-start | bytes 417800 | tf_op jit(solution)/shard_map/ppermute | solution.py:73
  17.5 1.6 %collective-permute-start.3 = (bf16[64,2176]{1,0:T(8,128)(2,1)S(1)}, bf16[64,2176]{1,0:T(8,128)(2,1)S(1)}, u32[]{:S(2)}, u32[]{:S(2)}) collective-permute-start(bf16[64,2176]{1,0:T(8,128)(2,1)S(1)} %pad_maximum_fusion.refs_0_), channel_id=1, source_target_pairs={{0,1},{1,0},{2,3},{3,2},{4,5},{5,4},{6,7},{7,6},{8,9},{9,8},{10,11... | collective-permute-start | bytes 835592 | tf_op jit(solution)/shard_map/ppermute | solution.py:73
  22.0 1.6 %collective-permute-start.4 = (bf16[64,2048]{1,0:T(8,128)(2,1)S(1)}, bf16[64,2048]{1,0:T(8,128)(2,1)S(1)}, u32[]{:S(2)}, u32[]{:S(2)}) collective-permute-start(bf16[64,2048]{1,0:T(8,128)(2,1)S(1)} %get-tuple-element.20), channel_id=1, source_target_pairs={{0,1},{1,0},{2,3},{3,2},{4,5},{5,4},{6,7},{7,6},{8,9},{9,8},{10,11... | collective-permute-start | bytes 786440 | tf_op jit(solution)/shard_map/ppermute | solution.py:73
  23.7 5.6 %collective-permute-start.5 = (bf16[32,2048]{1,0:T(8,128)(2,1)S(1)}, bf16[32,2048]{1,0:T(8,128)(2,1)S(1)}, u32[]{:S(2)}, u32[]{:S(2)}) collective-permute-start(bf16[32,2048]{1,0:T(8,128)(2,1)S(1)} %get-tuple-element.22), channel_id=1, source_target_pairs={{0,2},{1,3},{2,0},{3,1},{4,6},{5,7},{6,4},{7,5},{8,10},{9,11},{10,... | collective-permute-start | bytes 393224 | tf_op jit(solution)/shard_map/ppermute | solution.py:73
  29.3 4.3 %collective-permute-start.6 = (bf16[16,2048]{1,0:T(8,128)(2,1)S(1)}, bf16[16,2048]{1,0:T(8,128)(2,1)S(1)}, u32[]{:S(2)}, u32[]{:S(2)}) collective-permute-start(bf16[16,2048]{1,0:T(8,128)(2,1)S(1)} %get-tuple-element.24), channel_id=1, source_target_pairs={{0,4},{1,5},{2,6},{3,7},{4,0},{5,1},{6,2},{7,3},{8,12},{9,13},{10,... | collective-permute-start | bytes 196616 | tf_op jit(solution)/shard_map/ppermute | solution.py:73
  33.7 4.9 %collective-permute-start.7 = (bf16[8,2048]{1,0:T(8,128)(2,1)S(1)}, bf16[8,2048]{1,0:T(8,128)(2,1)S(1)}, u32[]{:S(2)}, u32[]{:S(2)}) collective-permute-start(bf16[8,2048]{1,0:T(8,128)(2,1)S(1)} %add_convert_fusion.5), channel_id=1, source_target_pairs={{0,8},{1,9},{2,10},{3,11},{4,12},{5,13},{6,14},{7,15},{8,0},{9,1},... | collective-permute-start | bytes 98312 | tf_op jit(solution)/shard_map/ppermute | solution.py:73

commit v3 on v2

--- a/solution.py
+++ b/solution.py
@@ -73,12 +73,16 @@
     return lax.ppermute(block, "expert", [(i, i ^ distance) for i in range(experts)])
 
 
-def joined(*blocks):
-    return lax.optimization_barrier(jnp.concatenate(blocks, axis=0))
-
-
-def add(a, b):
-    return (a.astype(jnp.float32) + b.astype(jnp.float32)).astype(jnp.bfloat16)
+def swap_apart(block, even, odd, experts):
+    return lax.ppermute(block, "expert", [(i, i ^ (odd if i % 2 else even)) for i in range(experts)])
+
+
+def joined(a, b, loaded):
+    return lax.optimization_barrier((jnp.concatenate([a, b], axis=0), loaded))
+
+
+def add(*blocks):
+    return functools.reduce(jnp.add, [block.astype(jnp.float32) for block in blocks]).astype(jnp.bfloat16)
 
 
 def pack_kernel(tokens_ref, share_ref, out_ref):
@@ -123,13 +127,16 @@
 
 def expert_kernel(experts, n_pieces, *refs):
     pieces = refs[:n_pieces]
-    mask_ref, gate_ref, up_ref, down_ref, keep_ref, send_ref, rows, hidden = refs[n_pieces:]
+    mask_ref, gate_ref, up_ref, down_ref = refs[n_pieces : n_pieces + 4]
+    answers = refs[n_pieces + 4 : 2 * n_pieces + 4]
+    rows, hidden = refs[2 * n_pieces + 4 :]
     width, units = gate_ref.shape[1:]
     me = lax.axis_index("expert")
-    spots = []
+    spots, spans = [], []
     at = 0
     for piece in pieces:
         count = piece.shape[0]
+        spans.append(slice(at, at + count))
         rows[at : at + count, :] = piece[:, :width]
         extra = piece[:, width:]
         lane = lax.broadcasted_iota(jnp.int32, extra.shape, 1)
@@ -144,55 +151,51 @@
         up_act = jnp.dot(rows[...], up_ref[0, :, cols], preferred_element_type=jnp.float32)
         value = gate_act / (1.0 + jnp.exp(-gate_act)) * up_act * keep
         hidden[:, cols] = value.astype(jnp.bfloat16)
-    half = rows.shape[0] // 2
     step = 512 if width % 512 == 0 else BLK
     for j in range(width // step):
         cols = slice(j * step, (j + 1) * step)
         answer = jnp.dot(hidden[...], down_ref[0, :, cols], preferred_element_type=jnp.float32)
         answer = (answer * share).astype(jnp.bfloat16)
-        keep_ref[:, cols] = answer[:half]
-        send_ref[:, cols] = answer[half:]
+        for answer_ref, span in zip(answers, spans):
+            answer_ref[:, cols] = answer[span]
 
 
 def dense_body(tokens, routes, combine, prune_mask, gate_weight, up_weight, down_weight):
     tok_dev, model_width = tokens.shape
     units = gate_weight.shape[2]
     experts = lax.axis_size("expert")
-    distances = [1 << bit for bit in range(experts.bit_length() - 1)]
     lanes = jnp.arange(3 * experts, dtype=jnp.int32) % experts
     chosen = routes[:, :, None] == lanes[None, None, :]
     shares = jnp.sum(jnp.where(chosen, combine[:, :, None], 0.0), axis=1)
-    rows = pl.pallas_call(
+    packed = pl.pallas_call(
         pack_kernel,
         out_shape=jax.ShapeDtypeStruct((tok_dev, model_width + BLK), jnp.bfloat16),
         in_specs=[WHOLE] * 2,
         out_specs=WHOLE,
         compiler_params=pltpu.CompilerParams(vmem_limit_bytes=1 << 20),
     )(tokens, shares)
-    weights = []
-    for distance, weight in zip(reversed(distances[1:]), (gate_weight, up_weight, down_weight)):
-        loaded = load(weight, rows)
-        both = jnp.concatenate([rows, swap(rows, distance, experts)], axis=0)
-        rows, loaded = lax.optimization_barrier((both, loaded))
-        weights.append(loaded)
-    pieces = [rows, swap(rows, distances[0], experts)]
+    own, gate_here = joined(packed, swap(packed, 8, experts), load(gate_weight, packed))
+    across = swap(own, 6, experts)
+    chip, up_here = joined(own, swap(own, 1, experts), load(up_weight, own))
+    beside = swap_apart(chip, 4, 2, experts)
+    beside, down_here = lax.optimization_barrier((beside, load(down_weight, chip)))
+    pieces = [chip, beside, across, swap(beside, 1, experts), swap(across, 1, experts)]
     total = sum(piece.shape[0] for piece in pieces)
-    out = jax.ShapeDtypeStruct((total // 2, model_width), jnp.bfloat16)
-    kept, sent = pl.pallas_call(
+    chip, beside, across, beside_far, across_far = pl.pallas_call(
         functools.partial(expert_kernel, experts, len(pieces)),
-        out_shape=(out, out),
+        out_shape=[jax.ShapeDtypeStruct((piece.shape[0], model_width), jnp.bfloat16) for piece in pieces],
         in_specs=[WHOLE] * len(pieces) + [pl.BlockSpec(memory_space=pltpu.SMEM)] + [WHOLE] * 3,
-        out_specs=(WHOLE, WHOLE),
+        out_specs=[WHOLE] * len(pieces),
         scratch_shapes=[pltpu.VMEM((total, model_width), jnp.bfloat16), pltpu.VMEM((total, units), jnp.bfloat16)],
         compiler_params=pltpu.CompilerParams(vmem_limit_bytes=16 << 20),
-    )(*pieces, prune_mask, *weights)
-    arrived = swap(sent, distances[0], experts)
-    for distance in distances[1:]:
-        half = kept.shape[0] // 2
-        sent = lax.optimization_barrier(add(kept[half:], arrived[half:]))
-        kept = add(kept[:half], arrived[:half])
-        arrived = swap(sent, distance, experts)
-    return add(kept, arrived)
+    )(*pieces, prune_mask, gate_here, up_here, down_here)
+    half = 2 * tok_dev
+    beside = swap_apart(lax.optimization_barrier(add(beside, swap(beside_far, 1, experts))), 4, 2, experts)
+    across = swap(lax.optimization_barrier(add(across, swap(across_far, 1, experts))), 6, experts)
+    far = swap(lax.optimization_barrier(add(chip[half:], beside[half:])), 1, experts)
+    near, beside, across = chip[:half], beside[:half], across
+    sent = lax.optimization_barrier(add(near[tok_dev:], beside[tok_dev:], across[tok_dev:], far[tok_dev:]))
+    return add(near[:tok_dev], beside[:tok_dev], across[:tok_dev], far[:tok_dev], swap(sent, 8, experts))
 
 
 def body(tokens, routes, combine, prune_mask, gate_weight, up_weight, down_weight):

time: 39.4 us -> 36.1 us (0.916)
  waiting for transfers between devices: 17.5 us -> 14 us
  local copies, waits for them, and re-layouts: 2.66 us -> 4.05 us
  starting transfers between devices: 13.7 us -> 12.5 us
    ppermute x8 -> x10, waiting for transfers between devices: 17.5 us -> 8.14 us  [swap(): lax.ppermute(block, 'expert', [(i, i ^ distance) for i in range(experts)])]
    ppermute x0 -> x2, waiting for transfers between devices: none -> 5.87 us  [swap_apart(): lax.ppermute(block, 'expert', [(i, i ^ (odd if i % 2 else even)) for i in...]
    ppermute x8 -> x10, starting transfers between devices: 13.7 us -> 9.32 us  [swap(): lax.ppermute(block, 'expert', [(i, i ^ distance) for i in range(experts)])]
    ppermute x0 -> x2, starting transfers between devices: none -> 3.18 us  [swap_apart(): lax.ppermute(block, 'expert', [(i, i ^ (odd if i % 2 else even)) for i in...]
    unnamed x10, local copies, waits for them, and re-layouts: 2.66 us -> 4.05 us
  transfers between devices with their start and end apart: 8 -> 12, of which waited for: 8 -> 9; matrix products, arithmetic and copies ran while one was open for 0% -> 0% of each run, Pallas kernels for 2% -> 2%
where the time goes in v3:
time: 36.1 us; the launch traced here: 35.9 us
  waiting for transfers between devices  14 us (39%)
  starting transfers between devices  12.5 us (35%)
  local copies, waits for them, and re-layouts  4.05 us (11%)
  Pallas kernels  3.64 us (10%)
  other arithmetic  1.55 us (4%)
    ppermute x10, starting transfers between devices, swap(): lax.ppermute(block, 'expert', [(i, i ^ distance) for i in range(experts)])  9.32 us
    ppermute x10, waiting for transfers between devices, swap(): lax.ppermute(block, 'expert', [(i, i ^ distance) for i in range(experts)])  8.14 us
    ppermute x2, waiting for transfers between devices, swap_apart(): lax.ppermute(block, 'expert', [(i, i ^ (odd if i % 2 else even)) for i in...  5.87 us
    unnamed x10, local copies, waits for them, and re-layouts  4.05 us
    ppermute x2, starting transfers between devices, swap_apart(): lax.ppermute(block, 'expert', [(i, i ^ (odd if i % 2 else even)) for i in...  3.18 us
    pallas_call x1, Pallas kernels, dense_body(): pl.pallas_call(functools.partial(expert_kernel, experts, len(pieces)), ou...  2.87 us
    reduce_sum x1, other arithmetic, dense_body(): shares = jnp.sum(jnp.where(chosen, combine[:, :, None], 0.0), axis=1)  0.79 us
    pallas_call x3, Pallas kernels, load(): pl.pallas_call(load_kernel, out_shape=jax.ShapeDtypeStruct(source.shape,...  0.76 us
  transfers between devices with their start and end apart: 12, of which 9 were waited for; matrix products, arithmetic and copies ran while one was open for 0% of the time, Pallas kernels for 2%

profile of v3, /device:TPU:0, one launch (start us, length us, event | category | flops | bytes accessed | tf_op | source)
XLA Modules:
  0.0 35.9 jit_solution(2422179092309832294)
XLA Ops:
  0.0 0.8 %select_reduce_fusion.share_ref = f32[8,48]{1,0:T(8,128)S(1)} fusion(f32[8,8]{1,0:T(8,128)} %param.9, s32[48]{0:T(128)S(1)} %and_select_fusion, s32[8,8]{1,0:T(8,128)} %param.8), kind=kLoop, calls=%fused_computation.7 | loop fusion | flops 8832 | bytes 2240 | tf_op jit(solution)/shard_map/reduce_sum | solution.py:169
  0.8 0.0 copy-start.3
  0.8 0.7 %copy-done.3 = bf16[8,2048]{1,0:T(8,128)(2,1)S(1)} copy-done((bf16[8,2048]{1,0:T(8,128)(2,1)S(1)}, bf16[8,2048]{1,0:T(8,128)(2,1)}, u32[]{:S(2)}) %copy-start.3) | copy-done | bytes 32792
  1.6 4.1 %collective-permute-start = (bf16[8,2176]{1,0:T(8,128)(2,1)S(1)}, bf16[8,2176]{1,0:T(8,128)(2,1)S(1)}, u32[]{:S(2)}, u32[]{:S(2)}) collective-permute-start(bf16[8,2176]{1,0:T(8,128)(2,1)S(1)} %shard_map.73.after), channel_id=1, source_target_pairs={{0,8},{1,9},{2,10},{3,11},{4,12},{5,13},{6,14},{7,15},{8,0},{9,1},... | collective-permute-start | bytes 104456 | tf_op jit(solution)/shard_map/ppermute | solution.py:73
  5.7 0.0 copy-start
  5.7 1.9 %copy-done = bf16[1,2048,768]{2,1,0:T(8,128)(2,1)S(1)} copy-done((bf16[1,2048,768]{2,1,0:T(8,128)(2,1)S(1)}, bf16[1,2048,768]{2,1,0:T(8,128)(2,1)}, u32[]{:S(2)}) %copy-start) | copy-done | bytes 3145752
  7.6 0.0 copy-start.2
  7.6 0.3 shard_map.74.refs_6_
  7.8 0.1 collective-permute-done
  8.0 0.0 copy-start.1
  8.0 0.1 collective-permute-start.1
  8.1 1.4 %copy-done.2 = bf16[1,2048,768]{2,1,0:T(8,128)(2,1)S(1)} copy-done((bf16[1,2048,768]{2,1,0:T(8,128)(2,1)S(1)}, bf16[1,2048,768]{2,1,0:T(8,128)(2,1)}, u32[]{:S(2)}) %copy-start.2) | copy-done | bytes 3145752
  9.5 0.3 shard_map.75.refs_7_
  9.7 0.0 collective-permute-done.1
  9.8 0.0 copy-start.4
  9.8 1.6 %collective-permute-start.2 = (bf16[32,2176]{1,0:T(8,128)(2,1)S(1)}, bf16[32,2176]{1,0:T(8,128)(2,1)S(1)}, u32[]{:S(2)}, u32[]{:S(2)}) collective-permute-start(bf16[32,2176]{1,0:T(8,128)(2,1)S(1)} %pad_maximum_fusion.after.refs_0_), channel_id=1, source_target_pairs={{0,4},{1,3},{2,6},{3,1},{4,0},{5,7},{6,2},{7,5},{8,12},{9,11},{10,... | collective-permute-start | bytes 417800 | tf_op jit(solution)/shard_map/ppermute | solution.py:77
  11.4 1.4 %collective-permute-start.3 = (bf16[16,2176]{1,0:T(8,128)(2,1)S(1)}, bf16[16,2176]{1,0:T(8,128)(2,1)S(1)}, u32[]{:S(2)}, u32[]{:S(2)}) collective-permute-start(bf16[16,2176]{1,0:T(8,128)(2,1)S(1)} %pad_maximum_fusion.1.after), channel_id=1, source_target_pairs={{0,6},{1,7},{2,4},{3,5},{4,2},{5,3},{6,0},{7,1},{8,14},{9,15},{10,... | collective-permute-start | bytes 208904 | tf_op jit(solution)/shard_map/ppermute | solution.py:73
  12.8 0.0 copy-done.1
  12.8 0.3 shard_map.76.refs_8_
  13.0 2.6 %collective-permute-done.2.refs_1_ = bf16[32,2176]{1,0:T(8,128)(2,1)S(1)} collective-permute-done((bf16[32,2176]{1,0:T(8,128)(2,1)S(1)}, bf16[32,2176]{1,0:T(8,128)(2,1)S(1)}, u32[]{:S(2)}, u32[]{:S(2)}) %collective-permute-start.2) | collective-permute-done | bytes 139296 | tf_op jit(solution)/shard_map/ppermute | solution.py:77
  15.6 0.0 collective-permute-start.4
  15.6 1.7 %collective-permute-done.3.refs_2_ = bf16[16,2176]{1,0:T(8,128)(2,1)S(1)} collective-permute-done((bf16[16,2176]{1,0:T(8,128)(2,1)S(1)}, bf16[16,2176]{1,0:T(8,128)(2,1)S(1)}, u32[]{:S(2)}, u32[]{:S(2)}) %collective-permute-start.3) | collective-permute-done | bytes 69664 | tf_op jit(solution)/shard_map/ppermute | solution.py:73
  17.3 0.0 collective-permute-start.5
  17.3 1.3 %collective-permute-done.5.refs_4_ = bf16[16,2176]{1,0:T(8,128)(2,1)S(1)} collective-permute-done((bf16[16,2176]{1,0:T(8,128)(2,1)S(1)}, bf16[16,2176]{1,0:T(8,128)(2,1)S(1)}, u32[]{:S(2)}, u32[]{:S(2)}) %collective-permute-start.5) | collective-permute-done | bytes 69664 | tf_op jit(solution)/shard_map/ppermute | solution.py:73
  18.6 0.0 collective-permute-done.4.refs_3_
  18.6 0.0 copy-done.4
  18.6 2.9 %shard_map.77 = (bf16[32,2048]{1,0:T(8,128)(2,1)S(1)}, bf16[32,2048]{1,0:T(8,128)(2,1)S(1)}, bf16[16,2048]{1,0:T(8,128)(2,1)S(1)}, bf16[32,2048]{1,0:T(8,128)(2,1)S(1)}, bf16[16,2048]{1,0:T(8,128)(2,1)S(1)}) custom-call(bf16[32,2176]{1,0:T(8,128)(2,1)S(1)} %pad_maximum_fusion.after.refs_0_, bf16[32,2176]{1,0:T(8,128)(2,1)S(1)} %collective-permute-done.2.refs_1_, ...), custom_call_target="tpu_custom_call" | custom-call | tf_op jit(solution)/shard_map/pallas_call | solution.py:184
  21.5 0.2 collective-permute-start.6
  21.7 0.4 collective-permute-start.8
  22.0 0.8 %collective-permute-done.6 = bf16[32,2048]{1,0:T(8,128)(2,1)S(1)} collective-permute-done((bf16[32,2048]{1,0:T(8,128)(2,1)S(1)}, bf16[32,2048]{1,0:T(8,128)(2,1)S(1)}, u32[]{:S(2)}, u32[]{:S(2)}) %collective-permute-start.6) | collective-permute-done | bytes 131104 | tf_op jit(solution)/shard_map/ppermute | solution.py:73
  22.9 1.5 %collective-permute-start.7 = (bf16[32,2048]{1,0:T(8,128)(2,1)S(1)}, bf16[32,2048]{1,0:T(8,128)(2,1)S(1)}, u32[]{:S(2)}, u32[]{:S(2)}) collective-permute-start(bf16[32,2048]{1,0:T(8,128)(2,1)S(1)} %add_convert_fusion), channel_id=1, source_target_pairs={{0,4},{1,3},{2,6},{3,1},{4,0},{5,7},{6,2},{7,5},{8,12},{9,11},{10,... | collective-permute-start | bytes 393224 | tf_op jit(solution)/shard_map/ppermute | solution.py:77
  24.4 0.0 collective-permute-done.8
  24.5 0.9 %collective-permute-start.9 = (bf16[16,2048]{1,0:T(8,128)(2,1)S(1)}, bf16[16,2048]{1,0:T(8,128)(2,1)S(1)}, u32[]{:S(2)}, u32[]{:S(2)}) collective-permute-start(bf16[16,2048]{1,0:T(8,128)(2,1)S(1)} %add_convert_fusion.2), channel_id=1, source_target_pairs={{0,6},{1,7},{2,4},{3,5},{4,2},{5,3},{6,0},{7,1},{8,14},{9,15},{10,... | collective-permute-start | bytes 196616 | tf_op jit(solution)/shard_map/ppermute | solution.py:73
  25.3 3.3 %collective-permute-done.7 = bf16[32,2048]{1,0:T(8,128)(2,1)S(1)} collective-permute-done((bf16[32,2048]{1,0:T(8,128)(2,1)S(1)}, bf16[32,2048]{1,0:T(8,128)(2,1)S(1)}, u32[]{:S(2)}, u32[]{:S(2)}) %collective-permute-start.7) | collective-permute-done | bytes 131104 | tf_op jit(solution)/shard_map/ppermute | solution.py:77
  28.7 0.1 collective-permute-start.10
  28.7 1.0 %collective-permute-done.9 = bf16[16,2048]{1,0:T(8,128)(2,1)S(1)} collective-permute-done((bf16[16,2048]{1,0:T(8,128)(2,1)S(1)}, bf16[16,2048]{1,0:T(8,128)(2,1)S(1)}, u32[]{:S(2)}, u32[]{:S(2)}) %collective-permute-start.9) | collective-permute-done | bytes 65568 | tf_op jit(solution)/shard_map/ppermute | solution.py:73
  29.7 0.3 collective-permute-done.10
  30.0 2.3 %collective-permute-start.11 = (bf16[8,2048]{1,0:T(8,128)(2,1)S(1)}, bf16[8,2048]{1,0:T(8,128)(2,1)S(1)}, u32[]{:S(2)}, u32[]{:S(2)}) collective-permute-start(bf16[8,2048]{1,0:T(8,128)(2,1)S(1)} %add_convert_fusion.4), channel_id=1, source_target_pairs={{0,8},{1,9},{2,10},{3,11},{4,12},{5,13},{6,14},{7,15},{8,0},{9,1},... | collective-permute-start | bytes 98312 | tf_op jit(solution)/shard_map/ppermute | solution.py:73
  32.3 3.0 %collective-permute-done.11 = bf16[8,2048]{1,0:T(8,128)(2,1)S(1)} collective-permute-done((bf16[8,2048]{1,0:T(8,128)(2,1)S(1)}, bf16[8,2048]{1,0:T(8,128)(2,1)S(1)}, u32[]{:S(2)}, u32[]{:S(2)}) %collective-permute-start.11) | collective-permute-done | bytes 32800 | tf_op jit(solution)/shard_map/ppermute | solution.py:73
  35.2 0.6 %add_convert_fusion.3 = bf16[8,2048]{1,0:T(8,128)(2,1)} fusion(bf16[8,2048]{1,0:T(8,128)(2,1)S(1)} %collective-permute-done.11, bf16[16,2048]{1,0:T(8,128)(2,1)S(1)} %collective-permute-done.10, bf16[16,2048]{1,0:T(8,128)(2,1)S(1)} %collective-permute-done.9, bf16[32,2048]{1,0:T(8,128)(2,1)S(1)} %collective-permute-done.7, ...), kind=kLoop, calls=%fused_computation.5 | loop fusion | flops 163840 | bytes 196608 | tf_op jit(solution)/shard_map/convert_element_type | solution.py:85
  (8 shorter events, 0.1 us)
Async XLA Ops:
  0.8 0.8 %copy-start.3 = (bf16[8,2048]{1,0:T(8,128)(2,1)S(1)}, bf16[8,2048]{1,0:T(8,128)(2,1)}, u32[]{:S(2)}) copy-start(bf16[8,2048]{1,0:T(8,128)(2,1)} %tokens_ref.1) | copy-start | bytes 98308
  1.6 6.4 %collective-permute-start = (bf16[8,2176]{1,0:T(8,128)(2,1)S(1)}, bf16[8,2176]{1,0:T(8,128)(2,1)S(1)}, u32[]{:S(2)}, u32[]{:S(2)}) collective-permute-start(bf16[8,2176]{1,0:T(8,128)(2,1)S(1)} %shard_map.73.after), channel_id=1, source_target_pairs={{0,8},{1,9},{2,10},{3,11},{4,12},{5,13},{6,14},{7,15},{8,0},{9,1},... | collective-permute-start | bytes 104456 | tf_op jit(solution)/shard_map/ppermute | solution.py:73
  5.7 1.9 %copy-start = (bf16[1,2048,768]{2,1,0:T(8,128)(2,1)S(1)}, bf16[1,2048,768]{2,1,0:T(8,128)(2,1)}, u32[]{:S(2)}) copy-start(bf16[1,2048,768]{2,1,0:T(8,128)(2,1)} %source.3) | copy-start | bytes 9437188
  7.6 1.9 %copy-start.2 = (bf16[1,2048,768]{2,1,0:T(8,128)(2,1)S(1)}, bf16[1,2048,768]{2,1,0:T(8,128)(2,1)}, u32[]{:S(2)}) copy-start(bf16[1,2048,768]{2,1,0:T(8,128)(2,1)} %source.4) | copy-start | bytes 9437188
  8.0 4.8 %copy-start.1 = (bf16[1,768,2048]{2,1,0:T(8,128)(2,1)S(1)}, bf16[1,768,2048]{2,1,0:T(8,128)(2,1)}, u32[]{:S(2)}) copy-start(bf16[1,768,2048]{2,1,0:T(8,128)(2,1)} %source.5) | copy-start | bytes 9437188
  8.0 1.7 %collective-permute-start.1 = (bf16[16,2176]{1,0:T(8,128)(2,1)S(1)}, bf16[16,2176]{1,0:T(8,128)(2,1)S(1)}, u32[]{:S(2)}, u32[]{:S(2)}) collective-permute-start(bf16[16,2176]{1,0:T(8,128)(2,1)S(1)} %pad_maximum_fusion.1.after), channel_id=1, source_target_pairs={{0,1},{1,0},{2,3},{3,2},{4,5},{5,4},{6,7},{7,6},{8,9},{9,8},{10,11... | collective-permute-start | bytes 208904 | tf_op jit(solution)/shard_map/ppermute | solution.py:73
  9.8 8.8 %copy-start.4 = (s32[1,6]{1,0:T(1,128)S(1)}, s32[1,6]{1,0:T(1,128)}, u32[]{:S(2)}) copy-start(s32[1,6]{1,0:T(1,128)} %refs_5_.1) | copy-start | bytes 76
  9.8 5.8 %collective-permute-start.2 = (bf16[32,2176]{1,0:T(8,128)(2,1)S(1)}, bf16[32,2176]{1,0:T(8,128)(2,1)S(1)}, u32[]{:S(2)}, u32[]{:S(2)}) collective-permute-start(bf16[32,2176]{1,0:T(8,128)(2,1)S(1)} %pad_maximum_fusion.after.refs_0_), channel_id=1, source_target_pairs={{0,4},{1,3},{2,6},{3,1},{4,0},{5,7},{6,2},{7,5},{8,12},{9,11},{10,... | collective-permute-start | bytes 417800 | tf_op jit(solution)/shard_map/ppermute | solution.py:77
  11.4 5.9 %collective-permute-start.3 = (bf16[16,2176]{1,0:T(8,128)(2,1)S(1)}, bf16[16,2176]{1,0:T(8,128)(2,1)S(1)}, u32[]{:S(2)}, u32[]{:S(2)}) collective-permute-start(bf16[16,2176]{1,0:T(8,128)(2,1)S(1)} %pad_maximum_fusion.1.after), channel_id=1, source_target_pairs={{0,6},{1,7},{2,4},{3,5},{4,2},{5,3},{6,0},{7,1},{8,14},{9,15},{10,... | collective-permute-start | bytes 208904 | tf_op jit(solution)/shard_map/ppermute | solution.py:73
  15.6 3.0 %collective-permute-start.4 = (bf16[32,2176]{1,0:T(8,128)(2,1)S(1)}, bf16[32,2176]{1,0:T(8,128)(2,1)S(1)}, u32[]{:S(2)}, u32[]{:S(2)}) collective-permute-start(bf16[32,2176]{1,0:T(8,128)(2,1)S(1)} %collective-permute-done.2.refs_1_), channel_id=1, source_target_pairs={{0,1},{1,0},{2,3},{3,2},{4,5},{5,4},{6,7},{7,6},{8,9},{9,8},{10,11... | collective-permute-start | bytes 417800 | tf_op jit(solution)/shard_map/ppermute | solution.py:73
  17.3 1.3 %collective-permute-start.5 = (bf16[16,2176]{1,0:T(8,128)(2,1)S(1)}, bf16[16,2176]{1,0:T(8,128)(2,1)S(1)}, u32[]{:S(2)}, u32[]{:S(2)}) collective-permute-start(bf16[16,2176]{1,0:T(8,128)(2,1)S(1)} %collective-permute-done.3.refs_2_), channel_id=1, source_target_pairs={{0,1},{1,0},{2,3},{3,2},{4,5},{5,4},{6,7},{7,6},{8,9},{9,8},{10,11... | collective-permute-start | bytes 208904 | tf_op jit(solution)/shard_map/ppermute | solution.py:73
  21.5 1.4 %collective-permute-start.6 = (bf16[32,2048]{1,0:T(8,128)(2,1)S(1)}, bf16[32,2048]{1,0:T(8,128)(2,1)S(1)}, u32[]{:S(2)}, u32[]{:S(2)}) collective-permute-start(bf16[32,2048]{1,0:T(8,128)(2,1)S(1)} %get-tuple-element.24), channel_id=1, source_target_pairs={{0,1},{1,0},{2,3},{3,2},{4,5},{5,4},{6,7},{7,6},{8,9},{9,8},{10,11... | collective-permute-start | bytes 393224 | tf_op jit(solution)/shard_map/ppermute | solution.py:73
  21.7 2.8 %collective-permute-start.8 = (bf16[16,2048]{1,0:T(8,128)(2,1)S(1)}, bf16[16,2048]{1,0:T(8,128)(2,1)S(1)}, u32[]{:S(2)}, u32[]{:S(2)}) collective-permute-start(bf16[16,2048]{1,0:T(8,128)(2,1)S(1)} %get-tuple-element.26), channel_id=1, source_target_pairs={{0,1},{1,0},{2,3},{3,2},{4,5},{5,4},{6,7},{7,6},{8,9},{9,8},{10,11... | collective-permute-start | bytes 196616 | tf_op jit(solution)/shard_map/ppermute | solution.py:73
  22.9 5.7 %collective-permute-start.7 = (bf16[32,2048]{1,0:T(8,128)(2,1)S(1)}, bf16[32,2048]{1,0:T(8,128)(2,1)S(1)}, u32[]{:S(2)}, u32[]{:S(2)}) collective-permute-start(bf16[32,2048]{1,0:T(8,128)(2,1)S(1)} %add_convert_fusion), channel_id=1, source_target_pairs={{0,4},{1,3},{2,6},{3,1},{4,0},{5,7},{6,2},{7,5},{8,12},{9,11},{10,... | collective-permute-start | bytes 393224 | tf_op jit(solution)/shard_map/ppermute | solution.py:77
  24.5 5.2 %collective-permute-start.9 = (bf16[16,2048]{1,0:T(8,128)(2,1)S(1)}, bf16[16,2048]{1,0:T(8,128)(2,1)S(1)}, u32[]{:S(2)}, u32[]{:S(2)}) collective-permute-start(bf16[16,2048]{1,0:T(8,128)(2,1)S(1)} %add_convert_fusion.2), channel_id=1, source_target_pairs={{0,6},{1,7},{2,4},{3,5},{4,2},{5,3},{6,0},{7,1},{8,14},{9,15},{10,... | collective-permute-start | bytes 196616 | tf_op jit(solution)/shard_map/ppermute | solution.py:73
  28.7 1.3 %collective-permute-start.10 = (bf16[16,2048]{1,0:T(8,128)(2,1)S(1)}, bf16[16,2048]{1,0:T(8,128)(2,1)S(1)}, u32[]{:S(2)}, u32[]{:S(2)}) collective-permute-start(bf16[16,2048]{1,0:T(8,128)(2,1)S(1)} %add_convert_fusion.1), channel_id=1, source_target_pairs={{0,1},{1,0},{2,3},{3,2},{4,5},{5,4},{6,7},{7,6},{8,9},{9,8},{10,11... | collective-permute-start | bytes 196616 | tf_op jit(solution)/shard_map/ppermute | solution.py:73
  30.0 5.2 %collective-permute-start.11 = (bf16[8,2048]{1,0:T(8,128)(2,1)S(1)}, bf16[8,2048]{1,0:T(8,128)(2,1)S(1)}, u32[]{:S(2)}, u32[]{:S(2)}) collective-permute-start(bf16[8,2048]{1,0:T(8,128)(2,1)S(1)} %add_convert_fusion.4), channel_id=1, source_target_pairs={{0,8},{1,9},{2,10},{3,11},{4,12},{5,13},{6,14},{7,15},{8,0},{9,1},... | collective-permute-start | bytes 98312 | tf_op jit(solution)/shard_map/ppermute | solution.py:73

commit v4 on v3

--- a/solution.py
+++ b/solution.py
@@ -144,11 +144,15 @@
         spots.append(jnp.sum(jnp.where(mine, extra.astype(jnp.float32), 0.0), axis=1, keepdims=True))
         at += count
     share = jnp.concatenate(spots, axis=0)
-    for j in range(units // BLK):
-        cols = slice(j * BLK, (j + 1) * BLK)
-        keep = mask_ref[0, j].astype(jnp.float32)
+    wide = 2 * BLK if units % (2 * BLK) == 0 else BLK
+    for j in range(units // wide):
+        cols = slice(j * wide, (j + 1) * wide)
         gate_act = jnp.dot(rows[...], gate_ref[0, :, cols], preferred_element_type=jnp.float32)
         up_act = jnp.dot(rows[...], up_ref[0, :, cols], preferred_element_type=jnp.float32)
+        block = lax.broadcasted_iota(jnp.int32, (1, wide), 1) // BLK
+        keep = jnp.zeros((1, wide), jnp.float32)
+        for i in range(wide // BLK):
+            keep = jnp.where(block == i, mask_ref[0, j * (wide // BLK) + i].astype(jnp.float32), keep)
         value = gate_act / (1.0 + jnp.exp(-gate_act)) * up_act * keep
         hidden[:, cols] = value.astype(jnp.bfloat16)
     step = 512 if width % 512 == 0 else BLK
@@ -175,13 +179,12 @@
         compiler_params=pltpu.CompilerParams(vmem_limit_bytes=1 << 20),
     )(tokens, shares)
     own, gate_here = joined(packed, swap(packed, 8, experts), load(gate_weight, packed))
-    across = swap(own, 6, experts)
-    chip, up_here = joined(own, swap(own, 1, experts), load(up_weight, own))
-    beside = swap_apart(chip, 4, 2, experts)
-    beside, down_here = lax.optimization_barrier((beside, load(down_weight, chip)))
-    pieces = [chip, beside, across, swap(beside, 1, experts), swap(across, 1, experts)]
+    arrived = [swap(own, distance, experts) for distance in (2, 6, 4)]
+    here = [own, *arrived]
+    *here, up_here, down_here = lax.optimization_barrier((*here, load(up_weight, own), load(down_weight, own)))
+    pieces = here + [swap(block, 1, experts) for block in here]
     total = sum(piece.shape[0] for piece in pieces)
-    chip, beside, across, beside_far, across_far = pl.pallas_call(
+    answers = pl.pallas_call(
         functools.partial(expert_kernel, experts, len(pieces)),
         out_shape=[jax.ShapeDtypeStruct((piece.shape[0], model_width), jnp.bfloat16) for piece in pieces],
         in_specs=[WHOLE] * len(pieces) + [pl.BlockSpec(memory_space=pltpu.SMEM)] + [WHOLE] * 3,
@@ -189,13 +192,12 @@
         scratch_shapes=[pltpu.VMEM((total, model_width), jnp.bfloat16), pltpu.VMEM((total, units), jnp.bfloat16)],
         compiler_params=pltpu.CompilerParams(vmem_limit_bytes=16 << 20),
     )(*pieces, prune_mask, gate_here, up_here, down_here)
-    half = 2 * tok_dev
-    beside = swap_apart(lax.optimization_barrier(add(beside, swap(beside_far, 1, experts))), 4, 2, experts)
-    across = swap(lax.optimization_barrier(add(across, swap(across_far, 1, experts))), 6, experts)
-    far = swap(lax.optimization_barrier(add(chip[half:], beside[half:])), 1, experts)
-    near, beside, across = chip[:half], beside[:half], across
-    sent = lax.optimization_barrier(add(near[tok_dev:], beside[tok_dev:], across[tok_dev:], far[tok_dev:]))
-    return add(near[:tok_dev], beside[:tok_dev], across[:tok_dev], far[:tok_dev], swap(sent, 8, experts))
+    count = len(here)
+    sums = [add(mine, swap(other, 1, experts)) for mine, other in zip(answers[:count], answers[count:])]
+    sums = sums[:1] + [lax.optimization_barrier(block) for block in sums[1:]]
+    terms = sums[:1] + [swap(block, distance, experts) for block, distance in zip(sums[1:], (2, 6, 4))]
+    sent = lax.optimization_barrier(add(*[term[tok_dev:] for term in terms]))
+    return add(*[term[:tok_dev] for term in terms], swap(sent, 8, experts))
 
 
 def body(tokens, routes, combine, prune_mask, gate_weight, up_weight, down_weight):

time: 36.1 us -> 34 us (0.942)
  starting transfers between devices: 12.5 us -> 16.4 us
  waiting for transfers between devices: 14 us -> 10.2 us
  local copies, waits for them, and re-layouts: 4.05 us -> 2.66 us
  Pallas kernels: 3.64 us -> 2.84 us
    ppermute x10 -> x16, starting transfers between devices: 9.32 us -> 16.4 us  [swap(): lax.ppermute(block, 'expert', [(i, i ^ distance) for i in range(experts)])]
    ppermute x2 -> x0, waiting for transfers between devices: 5.87 us -> none  [swap_apart(): lax.ppermute(block, 'expert', [(i, i ^ (odd if i % 2 else even)) for i in...]
    ppermute x2 -> x0, starting transfers between devices: 3.18 us -> none  [swap_apart(): lax.ppermute(block, 'expert', [(i, i ^ (odd if i % 2 else even)) for i in...]
    ppermute x10 -> x16, waiting for transfers between devices: 8.14 us -> 10.2 us  [swap(): lax.ppermute(block, 'expert', [(i, i ^ distance) for i in range(experts)])]
    unnamed x10, local copies, waits for them, and re-layouts: 4.05 us -> 2.66 us
    pallas_call x1, Pallas kernels: 2.87 us -> 2.07 us  [dense_body(): pl.pallas_call(functools.partial(expert_kernel, experts, len(pieces)), ou...]
    convert_element_type x5 -> x6, other arithmetic: 0.73 us -> 0.73 us  [add(): functools.reduce(jnp.add, [block.astype(jnp.float32) for block in blocks])]
  transfers between devices with their start and end apart: 12 -> 16, of which waited for: 9 -> 13; matrix products, arithmetic and copies ran while one was open for 0% -> 0% of each run, Pallas kernels for 2% -> 2%
where the time goes in v4:
time: 34 us; the launch traced here: 33.7 us
  starting transfers between devices  16.4 us (48%)
  waiting for transfers between devices  10.2 us (30%)
  Pallas kernels  2.84 us (8%)
  local copies, waits for them, and re-layouts  2.66 us (8%)
  other arithmetic  1.54 us (5%)
    ppermute x16, starting transfers between devices, swap(): lax.ppermute(block, 'expert', [(i, i ^ distance) for i in range(experts)])  16.4 us
    ppermute x16, waiting for transfers between devices, swap(): lax.ppermute(block, 'expert', [(i, i ^ distance) for i in range(experts)])  10.2 us
    unnamed x10, local copies, waits for them, and re-layouts  2.66 us
    pallas_call x1, Pallas kernels, dense_body(): pl.pallas_call(functools.partial(expert_kernel, experts, len(pieces)), ou...  2.07 us
    reduce_sum x1, other arithmetic, dense_body(): shares = jnp.sum(jnp.where(chosen, combine[:, :, None], 0.0), axis=1)  0.79 us
    pallas_call x3, Pallas kernels, load(): pl.pallas_call(load_kernel, out_shape=jax.ShapeDtypeStruct(source.shape,...  0.76 us
    convert_element_type x6, other arithmetic, add(): functools.reduce(jnp.add, [block.astype(jnp.float32) for block in blocks])  0.73 us
  transfers between devices with their start and end apart: 16, of which 13 were waited for; matrix products, arithmetic and copies ran while one was open for 0% of the time, Pallas kernels for 2%

profile of v4, /device:TPU:0, one launch (start us, length us, event | category | flops | bytes accessed | tf_op | source)
XLA Modules:
  0.0 33.7 jit_solution(6321048770499067300)
XLA Ops:
  0.0 0.8 %select_reduce_fusion.share_ref = f32[8,48]{1,0:T(8,128)S(1)} fusion(f32[8,8]{1,0:T(8,128)} %param.9, s32[48]{0:T(128)S(1)} %and_select_fusion, s32[8,8]{1,0:T(8,128)} %param.8), kind=kLoop, calls=%fused_computation.7 | loop fusion | flops 8832 | bytes 2240 | tf_op jit(solution)/shard_map/reduce_sum | solution.py:173
  0.8 0.0 copy-start.3
  0.8 0.7 %copy-done.3 = bf16[8,2048]{1,0:T(8,128)(2,1)S(1)} copy-done((bf16[8,2048]{1,0:T(8,128)(2,1)S(1)}, bf16[8,2048]{1,0:T(8,128)(2,1)}, u32[]{:S(2)}) %copy-start.3) | copy-done | bytes 32792
  1.6 4.1 %collective-permute-start = (bf16[8,2176]{1,0:T(8,128)(2,1)S(1)}, bf16[8,2176]{1,0:T(8,128)(2,1)S(1)}, u32[]{:S(2)}, u32[]{:S(2)}) collective-permute-start(bf16[8,2176]{1,0:T(8,128)(2,1)S(1)} %shard_map.73.after), channel_id=1, source_target_pairs={{0,8},{1,9},{2,10},{3,11},{4,12},{5,13},{6,14},{7,15},{8,0},{9,1},... | collective-permute-start | bytes 104456 | tf_op jit(solution)/shard_map/ppermute | solution.py:73
  5.7 0.0 copy-start
  5.7 1.9 %copy-done = bf16[1,2048,768]{2,1,0:T(8,128)(2,1)S(1)} copy-done((bf16[1,2048,768]{2,1,0:T(8,128)(2,1)S(1)}, bf16[1,2048,768]{2,1,0:T(8,128)(2,1)}, u32[]{:S(2)}) %copy-start) | copy-done | bytes 3145752
  7.6 0.0 copy-start.1
  7.6 0.3 shard_map.74.refs_9_
  7.8 0.1 collective-permute-done
  8.0 0.0 copy-start.2
  8.0 1.6 %collective-permute-start.3 = (bf16[16,2176]{1,0:T(8,128)(2,1)S(1)}, bf16[16,2176]{1,0:T(8,128)(2,1)S(1)}, u32[]{:S(2)}, u32[]{:S(2)}) collective-permute-start(bf16[16,2176]{1,0:T(8,128)(2,1)S(1)} %pad_maximum_fusion.after.refs_0_), channel_id=1, source_target_pairs={{0,4},{1,5},{2,6},{3,7},{4,0},{5,1},{6,2},{7,3},{8,12},{9,13},{10,... | collective-permute-start | bytes 208904 | tf_op jit(solution)/shard_map/ppermute | solution.py:73
  9.6 1.6 %collective-permute-start.2 = (bf16[16,2176]{1,0:T(8,128)(2,1)S(1)}, bf16[16,2176]{1,0:T(8,128)(2,1)S(1)}, u32[]{:S(2)}, u32[]{:S(2)}) collective-permute-start(bf16[16,2176]{1,0:T(8,128)(2,1)S(1)} %pad_maximum_fusion.after.refs_0_), channel_id=1, source_target_pairs={{0,6},{1,7},{2,4},{3,5},{4,2},{5,3},{6,0},{7,1},{8,14},{9,15},{10,... | collective-permute-start | bytes 208904 | tf_op jit(solution)/shard_map/ppermute | solution.py:73
  11.2 0.3 collective-permute-start.1
  11.5 0.0 copy-done.1
  11.5 0.3 shard_map.76.refs_11_
  11.8 0.0 copy-done.2
  11.8 0.0 copy-start.4
  11.8 0.3 shard_map.75.refs_10_
  12.1 0.4 %collective-permute-done.3.refs_3_ = bf16[16,2176]{1,0:T(8,128)(2,1)S(1)} collective-permute-done((bf16[16,2176]{1,0:T(8,128)(2,1)S(1)}, bf16[16,2176]{1,0:T(8,128)(2,1)S(1)}, u32[]{:S(2)}, u32[]{:S(2)}) %collective-permute-start.3) | collective-permute-done | bytes 69664 | tf_op jit(solution)/shard_map/ppermute | solution.py:73
  12.4 2.3 %collective-permute-done.2.refs_2_ = bf16[16,2176]{1,0:T(8,128)(2,1)S(1)} collective-permute-done((bf16[16,2176]{1,0:T(8,128)(2,1)S(1)}, bf16[16,2176]{1,0:T(8,128)(2,1)S(1)}, u32[]{:S(2)}, u32[]{:S(2)}) %collective-permute-start.2) | collective-permute-done | bytes 69664 | tf_op jit(solution)/shard_map/ppermute | solution.py:73
  14.8 0.7 %collective-permute-done.1.refs_1_ = bf16[16,2176]{1,0:T(8,128)(2,1)S(1)} collective-permute-done((bf16[16,2176]{1,0:T(8,128)(2,1)S(1)}, bf16[16,2176]{1,0:T(8,128)(2,1)S(1)}, u32[]{:S(2)}, u32[]{:S(2)}) %collective-permute-start.1) | collective-permute-done | bytes 69664 | tf_op jit(solution)/shard_map/ppermute | solution.py:73
  15.5 0.0 collective-permute-start.4
  15.5 0.5 %collective-permute-start.5 = (bf16[16,2176]{1,0:T(8,128)(2,1)S(1)}, bf16[16,2176]{1,0:T(8,128)(2,1)S(1)}, u32[]{:S(2)}, u32[]{:S(2)}) collective-permute-start(bf16[16,2176]{1,0:T(8,128)(2,1)S(1)} %collective-permute-done.1.refs_1_), channel_id=1, source_target_pairs={{0,1},{1,0},{2,3},{3,2},{4,5},{5,4},{6,7},{7,6},{8,9},{9,8},{10,11... | collective-permute-start | bytes 208904 | tf_op jit(solution)/shard_map/ppermute | solution.py:73
  16.0 0.0 collective-permute-start.6
  16.1 0.5 %collective-permute-start.7 = (bf16[16,2176]{1,0:T(8,128)(2,1)S(1)}, bf16[16,2176]{1,0:T(8,128)(2,1)S(1)}, u32[]{:S(2)}, u32[]{:S(2)}) collective-permute-start(bf16[16,2176]{1,0:T(8,128)(2,1)S(1)} %collective-permute-done.3.refs_3_), channel_id=1, source_target_pairs={{0,1},{1,0},{2,3},{3,2},{4,5},{5,4},{6,7},{7,6},{8,9},{9,8},{10,11... | collective-permute-start | bytes 208904 | tf_op jit(solution)/shard_map/ppermute | solution.py:73
  16.6 0.2 collective-permute-done.4.refs_4_
  16.8 0.2 collective-permute-done.5.refs_5_
  17.0 0.4 %collective-permute-done.6.refs_6_ = bf16[16,2176]{1,0:T(8,128)(2,1)S(1)} collective-permute-done((bf16[16,2176]{1,0:T(8,128)(2,1)S(1)}, bf16[16,2176]{1,0:T(8,128)(2,1)S(1)}, u32[]{:S(2)}, u32[]{:S(2)}) %collective-permute-start.6) | collective-permute-done | bytes 69664 | tf_op jit(solution)/shard_map/ppermute | solution.py:73
  17.3 0.2 collective-permute-done.7.refs_7_
  17.5 0.0 copy-done.4
  17.5 2.1 %shard_map.77 = (bf16[16,2048]{1,0:T(8,128)(2,1)S(1)}, bf16[16,2048]{1,0:T(8,128)(2,1)S(1)}, bf16[16,2048]{1,0:T(8,128)(2,1)S(1)}, bf16[16,2048]{1,0:T(8,128)(2,...) custom-call(bf16[16,2176]{1,0:T(8,128)(2,1)S(1)} %pad_maximum_fusion, ...), custom_call_target="tpu_custom_call" | custom-call | tf_op jit(solution)/shard_map/pallas_call | solution.py:187
  19.5 0.4 %collective-permute-start.9 = (bf16[16,2048]{1,0:T(8,128)(2,1)S(1)}, bf16[16,2048]{1,0:T(8,128)(2,1)S(1)}, u32[]{:S(2)}, u32[]{:S(2)}) collective-permute-start(bf16[16,2048]{1,0:T(8,128)(2,1)S(1)} %get-tuple-element.32), channel_id=1, source_target_pairs={{0,1},{1,0},{2,3},{3,2},{4,5},{5,4},{6,7},{7,6},{8,9},{9,8},{10,11... | collective-permute-start | bytes 196616 | tf_op jit(solution)/shard_map/ppermute | solution.py:73
  20.0 0.2 collective-permute-start.8
  20.1 0.4 %collective-permute-start.11 = (bf16[16,2048]{1,0:T(8,128)(2,1)S(1)}, bf16[16,2048]{1,0:T(8,128)(2,1)S(1)}, u32[]{:S(2)}, u32[]{:S(2)}) collective-permute-start(bf16[16,2048]{1,0:T(8,128)(2,1)S(1)} %get-tuple-element.34), channel_id=1, source_target_pairs={{0,1},{1,0},{2,3},{3,2},{4,5},{5,4},{6,7},{7,6},{8,9},{9,8},{10,11... | collective-permute-start | bytes 196616 | tf_op jit(solution)/shard_map/ppermute | solution.py:73
  20.5 0.2 collective-permute-start.13
  20.6 0.2 collective-permute-done.9
  20.9 1.1 %collective-permute-start.10 = (bf16[16,2048]{1,0:T(8,128)(2,1)S(1)}, bf16[16,2048]{1,0:T(8,128)(2,1)S(1)}, u32[]{:S(2)}, u32[]{:S(2)}) collective-permute-start(bf16[16,2048]{1,0:T(8,128)(2,1)S(1)} %add_convert_fusion.2), channel_id=1, source_target_pairs={{0,2},{1,3},{2,0},{3,1},{4,6},{5,7},{6,4},{7,5},{8,10},{9,11},{10,... | collective-permute-start | bytes 196616 | tf_op jit(solution)/shard_map/ppermute | solution.py:73
  22.0 0.0 collective-permute-done.11
  22.0 1.8 %collective-permute-start.12 = (bf16[16,2048]{1,0:T(8,128)(2,1)S(1)}, bf16[16,2048]{1,0:T(8,128)(2,1)S(1)}, u32[]{:S(2)}, u32[]{:S(2)}) collective-permute-start(bf16[16,2048]{1,0:T(8,128)(2,1)S(1)} %add_convert_fusion.1), channel_id=1, source_target_pairs={{0,6},{1,7},{2,4},{3,5},{4,2},{5,3},{6,0},{7,1},{8,14},{9,15},{10,... | collective-permute-start | bytes 196616 | tf_op jit(solution)/shard_map/ppermute | solution.py:73
  23.8 0.0 collective-permute-done.13
  23.8 0.8 %collective-permute-start.14 = (bf16[16,2048]{1,0:T(8,128)(2,1)S(1)}, bf16[16,2048]{1,0:T(8,128)(2,1)S(1)}, u32[]{:S(2)}, u32[]{:S(2)}) collective-permute-start(bf16[16,2048]{1,0:T(8,128)(2,1)S(1)} %add_convert_fusion), channel_id=1, source_target_pairs={{0,4},{1,5},{2,6},{3,7},{4,0},{5,1},{6,2},{7,3},{8,12},{9,13},{10,... | collective-permute-start | bytes 196616 | tf_op jit(solution)/shard_map/ppermute | solution.py:73
  24.6 0.0 collective-permute-done.8
  24.7 0.7 %collective-permute-done.10 = bf16[16,2048]{1,0:T(8,128)(2,1)S(1)} collective-permute-done((bf16[16,2048]{1,0:T(8,128)(2,1)S(1)}, bf16[16,2048]{1,0:T(8,128)(2,1)S(1)}, u32[]{:S(2)}, u32[]{:S(2)}) %collective-permute-start.10) | collective-permute-done | bytes 65568 | tf_op jit(solution)/shard_map/ppermute | solution.py:73
  25.3 2.6 %collective-permute-done.12 = bf16[16,2048]{1,0:T(8,128)(2,1)S(1)} collective-permute-done((bf16[16,2048]{1,0:T(8,128)(2,1)S(1)}, bf16[16,2048]{1,0:T(8,128)(2,1)S(1)}, u32[]{:S(2)}, u32[]{:S(2)}) %collective-permute-start.12) | collective-permute-done | bytes 65568 | tf_op jit(solution)/shard_map/ppermute | solution.py:73
  27.9 0.3 collective-permute-done.14
  28.2 2.9 %collective-permute-start.15 = (bf16[8,2048]{1,0:T(8,128)(2,1)S(1)}, bf16[8,2048]{1,0:T(8,128)(2,1)S(1)}, u32[]{:S(2)}, u32[]{:S(2)}) collective-permute-start(bf16[8,2048]{1,0:T(8,128)(2,1)S(1)} %add_convert_fusion.5), channel_id=1, source_target_pairs={{0,8},{1,9},{2,10},{3,11},{4,12},{5,13},{6,14},{7,15},{8,0},{9,1},... | collective-permute-start | bytes 98312 | tf_op jit(solution)/shard_map/ppermute | solution.py:73
  31.1 2.0 %collective-permute-done.15 = bf16[8,2048]{1,0:T(8,128)(2,1)S(1)} collective-permute-done((bf16[8,2048]{1,0:T(8,128)(2,1)S(1)}, bf16[8,2048]{1,0:T(8,128)(2,1)S(1)}, u32[]{:S(2)}, u32[]{:S(2)}) %collective-permute-start.15) | collective-permute-done | bytes 32800 | tf_op jit(solution)/shard_map/ppermute | solution.py:73
  33.1 0.6 %add_convert_fusion.4 = bf16[8,2048]{1,0:T(8,128)(2,1)} fusion(bf16[8,2048]{1,0:T(8,128)(2,1)S(1)} %collective-permute-done.15, bf16[16,2048]{1,0:T(8,128)(2,1)S(1)} %collective-permute-done.14, bf16[16,2048]{1,0:T(8,128)(2,1)S(1)} %collective-permute-done.12, bf16[16,2048]{1,0:T(8,128)(2,1)S(1)} %collective-permute-done.10, ...), kind=kLoop, calls=%fused_computation.5 | loop fusion | flops 163840 | bytes 196608 | tf_op jit(solution)/shard_map/convert_element_type | solution.py:85
  (8 shorter events, 0.1 us)
Async XLA Ops:
  0.8 0.8 %copy-start.3 = (bf16[8,2048]{1,0:T(8,128)(2,1)S(1)}, bf16[8,2048]{1,0:T(8,128)(2,1)}, u32[]{:S(2)}) copy-start(bf16[8,2048]{1,0:T(8,128)(2,1)} %tokens_ref.1) | copy-start | bytes 98308
  1.6 6.4 %collective-permute-start = (bf16[8,2176]{1,0:T(8,128)(2,1)S(1)}, bf16[8,2176]{1,0:T(8,128)(2,1)S(1)}, u32[]{:S(2)}, u32[]{:S(2)}) collective-permute-start(bf16[8,2176]{1,0:T(8,128)(2,1)S(1)} %shard_map.73.after), channel_id=1, source_target_pairs={{0,8},{1,9},{2,10},{3,11},{4,12},{5,13},{6,14},{7,15},{8,0},{9,1},... | collective-permute-start | bytes 104456 | tf_op jit(solution)/shard_map/ppermute | solution.py:73
  5.7 1.9 %copy-start = (bf16[1,2048,768]{2,1,0:T(8,128)(2,1)S(1)}, bf16[1,2048,768]{2,1,0:T(8,128)(2,1)}, u32[]{:S(2)}) copy-start(bf16[1,2048,768]{2,1,0:T(8,128)(2,1)} %source.3) | copy-start | bytes 9437188
  7.6 4.0 %copy-start.1 = (bf16[1,768,2048]{2,1,0:T(8,128)(2,1)S(1)}, bf16[1,768,2048]{2,1,0:T(8,128)(2,1)}, u32[]{:S(2)}) copy-start(bf16[1,768,2048]{2,1,0:T(8,128)(2,1)} %source.5) | copy-start | bytes 9437188
  8.0 3.8 %copy-start.2 = (bf16[1,2048,768]{2,1,0:T(8,128)(2,1)S(1)}, bf16[1,2048,768]{2,1,0:T(8,128)(2,1)}, u32[]{:S(2)}) copy-start(bf16[1,2048,768]{2,1,0:T(8,128)(2,1)} %source.4) | copy-start | bytes 9437188
  8.0 4.5 %collective-permute-start.3 = (bf16[16,2176]{1,0:T(8,128)(2,1)S(1)}, bf16[16,2176]{1,0:T(8,128)(2,1)S(1)}, u32[]{:S(2)}, u32[]{:S(2)}) collective-permute-start(bf16[16,2176]{1,0:T(8,128)(2,1)S(1)} %pad_maximum_fusion.after.refs_0_), channel_id=1, source_target_pairs={{0,4},{1,5},{2,6},{3,7},{4,0},{5,1},{6,2},{7,3},{8,12},{9,13},{10,... | collective-permute-start | bytes 208904 | tf_op jit(solution)/shard_map/ppermute | solution.py:73
  9.6 5.2 %collective-permute-start.2 = (bf16[16,2176]{1,0:T(8,128)(2,1)S(1)}, bf16[16,2176]{1,0:T(8,128)(2,1)S(1)}, u32[]{:S(2)}, u32[]{:S(2)}) collective-permute-start(bf16[16,2176]{1,0:T(8,128)(2,1)S(1)} %pad_maximum_fusion.after.refs_0_), channel_id=1, source_target_pairs={{0,6},{1,7},{2,4},{3,5},{4,2},{5,3},{6,0},{7,1},{8,14},{9,15},{10,... | collective-permute-start | bytes 208904 | tf_op jit(solution)/shard_map/ppermute | solution.py:73
  11.2 4.3 %collective-permute-start.1 = (bf16[16,2176]{1,0:T(8,128)(2,1)S(1)}, bf16[16,2176]{1,0:T(8,128)(2,1)S(1)}, u32[]{:S(2)}, u32[]{:S(2)}) collective-permute-start(bf16[16,2176]{1,0:T(8,128)(2,1)S(1)} %pad_maximum_fusion.after.refs_0_), channel_id=1, source_target_pairs={{0,2},{1,3},{2,0},{3,1},{4,6},{5,7},{6,4},{7,5},{8,10},{9,11},{10,... | collective-permute-start | bytes 208904 | tf_op jit(solution)/shard_map/ppermute | solution.py:73
  11.8 5.7 %copy-start.4 = (s32[1,6]{1,0:T(1,128)S(1)}, s32[1,6]{1,0:T(1,128)}, u32[]{:S(2)}) copy-start(s32[1,6]{1,0:T(1,128)} %refs_8_.1) | copy-start | bytes 76
  15.5 1.3 %collective-permute-start.4 = (bf16[16,2176]{1,0:T(8,128)(2,1)S(1)}, bf16[16,2176]{1,0:T(8,128)(2,1)S(1)}, u32[]{:S(2)}, u32[]{:S(2)}) collective-permute-start(bf16[16,2176]{1,0:T(8,128)(2,1)S(1)} %pad_maximum_fusion.after.refs_0_), channel_id=1, source_target_pairs={{0,1},{1,0},{2,3},{3,2},{4,5},{5,4},{6,7},{7,6},{8,9},{9,8},{10,11... | collective-permute-start | bytes 208904 | tf_op jit(solution)/shard_map/ppermute | solution.py:73
  15.5 1.4 %collective-permute-start.5 = (bf16[16,2176]{1,0:T(8,128)(2,1)S(1)}, bf16[16,2176]{1,0:T(8,128)(2,1)S(1)}, u32[]{:S(2)}, u32[]{:S(2)}) collective-permute-start(bf16[16,2176]{1,0:T(8,128)(2,1)S(1)} %collective-permute-done.1.refs_1_), channel_id=1, source_target_pairs={{0,1},{1,0},{2,3},{3,2},{4,5},{5,4},{6,7},{7,6},{8,9},{9,8},{10,11... | collective-permute-start | bytes 208904 | tf_op jit(solution)/shard_map/ppermute | solution.py:73
  16.0 1.3 %collective-permute-start.6 = (bf16[16,2176]{1,0:T(8,128)(2,1)S(1)}, bf16[16,2176]{1,0:T(8,128)(2,1)S(1)}, u32[]{:S(2)}, u32[]{:S(2)}) collective-permute-start(bf16[16,2176]{1,0:T(8,128)(2,1)S(1)} %collective-permute-done.2.refs_2_), channel_id=1, source_target_pairs={{0,1},{1,0},{2,3},{3,2},{4,5},{5,4},{6,7},{7,6},{8,9},{9,8},{10,11... | collective-permute-start | bytes 208904 | tf_op jit(solution)/shard_map/ppermute | solution.py:73
  16.1 1.4 %collective-permute-start.7 = (bf16[16,2176]{1,0:T(8,128)(2,1)S(1)}, bf16[16,2176]{1,0:T(8,128)(2,1)S(1)}, u32[]{:S(2)}, u32[]{:S(2)}) collective-permute-start(bf16[16,2176]{1,0:T(8,128)(2,1)S(1)} %collective-permute-done.3.refs_3_), channel_id=1, source_target_pairs={{0,1},{1,0},{2,3},{3,2},{4,5},{5,4},{6,7},{7,6},{8,9},{9,8},{10,11... | collective-permute-start | bytes 208904 | tf_op jit(solution)/shard_map/ppermute | solution.py:73
  19.5 1.3 %collective-permute-start.9 = (bf16[16,2048]{1,0:T(8,128)(2,1)S(1)}, bf16[16,2048]{1,0:T(8,128)(2,1)S(1)}, u32[]{:S(2)}, u32[]{:S(2)}) collective-permute-start(bf16[16,2048]{1,0:T(8,128)(2,1)S(1)} %get-tuple-element.32), channel_id=1, source_target_pairs={{0,1},{1,0},{2,3},{3,2},{4,5},{5,4},{6,7},{7,6},{8,9},{9,8},{10,11... | collective-permute-start | bytes 196616 | tf_op jit(solution)/shard_map/ppermute | solution.py:73
  20.0 4.7 %collective-permute-start.8 = (bf16[16,2048]{1,0:T(8,128)(2,1)S(1)}, bf16[16,2048]{1,0:T(8,128)(2,1)S(1)}, u32[]{:S(2)}, u32[]{:S(2)}) collective-permute-start(bf16[16,2048]{1,0:T(8,128)(2,1)S(1)} %get-tuple-element.30), channel_id=1, source_target_pairs={{0,1},{1,0},{2,3},{3,2},{4,5},{5,4},{6,7},{7,6},{8,9},{9,8},{10,11... | collective-permute-start | bytes 196616 | tf_op jit(solution)/shard_map/ppermute | solution.py:73
  20.1 1.9 %collective-permute-start.11 = (bf16[16,2048]{1,0:T(8,128)(2,1)S(1)}, bf16[16,2048]{1,0:T(8,128)(2,1)S(1)}, u32[]{:S(2)}, u32[]{:S(2)}) collective-permute-start(bf16[16,2048]{1,0:T(8,128)(2,1)S(1)} %get-tuple-element.34), channel_id=1, source_target_pairs={{0,1},{1,0},{2,3},{3,2},{4,5},{5,4},{6,7},{7,6},{8,9},{9,8},{10,11... | collective-permute-start | bytes 196616 | tf_op jit(solution)/shard_map/ppermute | solution.py:73
  20.5 3.3 %collective-permute-start.13 = (bf16[16,2048]{1,0:T(8,128)(2,1)S(1)}, bf16[16,2048]{1,0:T(8,128)(2,1)S(1)}, u32[]{:S(2)}, u32[]{:S(2)}) collective-permute-start(bf16[16,2048]{1,0:T(8,128)(2,1)S(1)} %get-tuple-element.36), channel_id=1, source_target_pairs={{0,1},{1,0},{2,3},{3,2},{4,5},{5,4},{6,7},{7,6},{8,9},{9,8},{10,11... | collective-permute-start | bytes 196616 | tf_op jit(solution)/shard_map/ppermute | solution.py:73
  20.9 4.4 %collective-permute-start.10 = (bf16[16,2048]{1,0:T(8,128)(2,1)S(1)}, bf16[16,2048]{1,0:T(8,128)(2,1)S(1)}, u32[]{:S(2)}, u32[]{:S(2)}) collective-permute-start(bf16[16,2048]{1,0:T(8,128)(2,1)S(1)} %add_convert_fusion.2), channel_id=1, source_target_pairs={{0,2},{1,3},{2,0},{3,1},{4,6},{5,7},{6,4},{7,5},{8,10},{9,11},{10,... | collective-permute-start | bytes 196616 | tf_op jit(solution)/shard_map/ppermute | solution.py:73
  22.0 5.9 %collective-permute-start.12 = (bf16[16,2048]{1,0:T(8,128)(2,1)S(1)}, bf16[16,2048]{1,0:T(8,128)(2,1)S(1)}, u32[]{:S(2)}, u32[]{:S(2)}) collective-permute-start(bf16[16,2048]{1,0:T(8,128)(2,1)S(1)} %add_convert_fusion.1), channel_id=1, source_target_pairs={{0,6},{1,7},{2,4},{3,5},{4,2},{5,3},{6,0},{7,1},{8,14},{9,15},{10,... | collective-permute-start | bytes 196616 | tf_op jit(solution)/shard_map/ppermute | solution.py:73
  23.8 4.3 %collective-permute-start.14 = (bf16[16,2048]{1,0:T(8,128)(2,1)S(1)}, bf16[16,2048]{1,0:T(8,128)(2,1)S(1)}, u32[]{:S(2)}, u32[]{:S(2)}) collective-permute-start(bf16[16,2048]{1,0:T(8,128)(2,1)S(1)} %add_convert_fusion), channel_id=1, source_target_pairs={{0,4},{1,5},{2,6},{3,7},{4,0},{5,1},{6,2},{7,3},{8,12},{9,13},{10,... | collective-permute-start | bytes 196616 | tf_op jit(solution)/shard_map/ppermute | solution.py:73
  28.2 4.9 %collective-permute-start.15 = (bf16[8,2048]{1,0:T(8,128)(2,1)S(1)}, bf16[8,2048]{1,0:T(8,128)(2,1)S(1)}, u32[]{:S(2)}, u32[]{:S(2)}) collective-permute-start(bf16[8,2048]{1,0:T(8,128)(2,1)S(1)} %add_convert_fusion.5), channel_id=1, source_target_pairs={{0,8},{1,9},{2,10},{3,11},{4,12},{5,13},{6,14},{7,15},{8,0},{9,1},... | collective-permute-start | bytes 98312 | tf_op jit(solution)/shard_map/ppermute | solution.py:73

commit v5 on v4

--- a/solution.py
+++ b/solution.py
@@ -128,15 +128,13 @@
 def expert_kernel(experts, n_pieces, *refs):
     pieces = refs[:n_pieces]
     mask_ref, gate_ref, up_ref, down_ref = refs[n_pieces : n_pieces + 4]
-    answers = refs[n_pieces + 4 : 2 * n_pieces + 4]
-    rows, hidden = refs[2 * n_pieces + 4 :]
+    *answers, rows, hidden = refs[n_pieces + 4 :]
     width, units = gate_ref.shape[1:]
     me = lax.axis_index("expert")
-    spots, spans = [], []
+    spots = []
     at = 0
     for piece in pieces:
         count = piece.shape[0]
-        spans.append(slice(at, at + count))
         rows[at : at + count, :] = piece[:, :width]
         extra = piece[:, width:]
         lane = lax.broadcasted_iota(jnp.int32, extra.shape, 1)
@@ -160,8 +158,10 @@
         cols = slice(j * step, (j + 1) * step)
         answer = jnp.dot(hidden[...], down_ref[0, :, cols], preferred_element_type=jnp.float32)
         answer = (answer * share).astype(jnp.bfloat16)
-        for answer_ref, span in zip(answers, spans):
-            answer_ref[:, cols] = answer[span]
+        at = 0
+        for answer_ref in answers:
+            answer_ref[:, cols] = answer[at : at + answer_ref.shape[0]]
+            at += answer_ref.shape[0]
 
 
 def dense_body(tokens, routes, combine, prune_mask, gate_weight, up_weight, down_weight):
@@ -179,23 +179,33 @@
         compiler_params=pltpu.CompilerParams(vmem_limit_bytes=1 << 20),
     )(tokens, shares)
     own, gate_here = joined(packed, swap(packed, 8, experts), load(gate_weight, packed))
-    arrived = [swap(own, distance, experts) for distance in (2, 6, 4)]
-    here = [own, *arrived]
-    *here, up_here, down_here = lax.optimization_barrier((*here, load(up_weight, own), load(down_weight, own)))
-    pieces = here + [swap(block, 1, experts) for block in here]
+    order = (4, 2, 6)
+    arrived = {distance: swap(own, distance, experts) for distance in order}
+    own_far = swap(own, 1, experts)
+    last, first = order[0], order[2]
+    first_far = swap(arrived[first], 1, experts)
+    arrived[last], own_far, first_far, up_here, down_here = lax.optimization_barrier(
+        (arrived[last], own_far, first_far, load(up_weight, own), load(down_weight, own))
+    )
+    far = {distance: swap(arrived[distance], 1, experts) for distance in order[:2]}
+    far[first] = first_far
+    pieces = [own, *[arrived[d] for d in (2, 6, 4)], far[(2, 6, 4)[0]], own_far, *[far[d] for d in (2, 6, 4)[1:]]]
     total = sum(piece.shape[0] for piece in pieces)
-    answers = pl.pallas_call(
+    block = own.shape[0]
+    heights = [block] * 5 + [3 * block]
+    *mine, first_far, rest_far = pl.pallas_call(
         functools.partial(expert_kernel, experts, len(pieces)),
-        out_shape=[jax.ShapeDtypeStruct((piece.shape[0], model_width), jnp.bfloat16) for piece in pieces],
+        out_shape=[jax.ShapeDtypeStruct((height, model_width), jnp.bfloat16) for height in heights],
         in_specs=[WHOLE] * len(pieces) + [pl.BlockSpec(memory_space=pltpu.SMEM)] + [WHOLE] * 3,
-        out_specs=[WHOLE] * len(pieces),
+        out_specs=[WHOLE] * len(heights),
         scratch_shapes=[pltpu.VMEM((total, model_width), jnp.bfloat16), pltpu.VMEM((total, units), jnp.bfloat16)],
         compiler_params=pltpu.CompilerParams(vmem_limit_bytes=16 << 20),
     )(*pieces, prune_mask, gate_here, up_here, down_here)
-    count = len(here)
-    sums = [add(mine, swap(other, 1, experts)) for mine, other in zip(answers[:count], answers[count:])]
-    sums = sums[:1] + [lax.optimization_barrier(block) for block in sums[1:]]
-    terms = sums[:1] + [swap(block, distance, experts) for block, distance in zip(sums[1:], (2, 6, 4))]
+    first_far, rest_far = swap(first_far, 1, experts), swap(rest_far, 1, experts)
+    others = [rest_far[:block], first_far, rest_far[block : 2 * block], rest_far[2 * block :]]
+    sums = [add(here, there) for here, there in zip(mine, others)]
+    sums = sums[:1] + [lax.optimization_barrier(one) for one in sums[1:]]
+    terms = sums[:1] + [swap(one, distance, experts) for one, distance in zip(sums[1:], (2, 6, 4))]
     sent = lax.optimization_barrier(add(*[term[tok_dev:] for term in terms]))
     return add(*[term[:tok_dev] for term in terms], swap(sent, 8, experts))
 

time: 34 us -> 33.3 us (0.979)
  starting transfers between devices: 16.4 us -> 14.8 us
  waiting for transfers between devices: 10.2 us -> 11.1 us
    ppermute x16 -> x14, starting transfers between devices: 16.4 us -> 14.8 us  [swap(): lax.ppermute(block, 'expert', [(i, i ^ distance) for i in range(experts)])]
    ppermute x16 -> x14, waiting for transfers between devices: 10.2 us -> 11.1 us  [swap(): lax.ppermute(block, 'expert', [(i, i ^ distance) for i in range(experts)])]
    convert_element_type x6 -> x4, other arithmetic: 0.73 us -> 0.73 us  [add(): functools.reduce(jnp.add, [block.astype(jnp.float32) for block in blocks])]
  transfers between devices with their start and end apart: 16 -> 14, of which waited for: 13 -> 10; matrix products, arithmetic and copies ran while one was open for 0% -> 0% of each run, Pallas kernels for 2% -> 2%
where the time goes in v5:
time: 33.3 us; the launch traced here: 33 us
  starting transfers between devices  14.8 us (44%)
  waiting for transfers between devices  11.1 us (33%)
  Pallas kernels  2.84 us (9%)
  local copies, waits for them, and re-layouts  2.66 us (8%)
  other arithmetic  1.53 us (5%)
    ppermute x14, starting transfers between devices, swap(): lax.ppermute(block, 'expert', [(i, i ^ distance) for i in range(experts)])  14.8 us
    ppermute x14, waiting for transfers between devices, swap(): lax.ppermute(block, 'expert', [(i, i ^ distance) for i in range(experts)])  11.1 us
    unnamed x10, local copies, waits for them, and re-layouts  2.66 us
    pallas_call x1, Pallas kernels, dense_body(): pl.pallas_call(functools.partial(expert_kernel, experts, len(pieces)), ou...  2.06 us
    reduce_sum x1, other arithmetic, dense_body(): shares = jnp.sum(jnp.where(chosen, combine[:, :, None], 0.0), axis=1)  0.79 us
    pallas_call x3, Pallas kernels, load(): pl.pallas_call(load_kernel, out_shape=jax.ShapeDtypeStruct(source.shape,...  0.76 us
    convert_element_type x4, other arithmetic, add(): functools.reduce(jnp.add, [block.astype(jnp.float32) for block in blocks])  0.73 us
  transfers between devices with their start and end apart: 14, of which 10 were waited for; matrix products, arithmetic and copies ran while one was open for 0% of the time, Pallas kernels for 2%

profile of v5, /device:TPU:0, one launch (start us, length us, event | category | flops | bytes accessed | tf_op | source)
XLA Modules:
  0.0 33.0 jit_solution(9929658464282748366)
XLA Ops:
  0.0 0.8 %select_reduce_fusion.share_ref = f32[8,48]{1,0:T(8,128)S(1)} fusion(f32[8,8]{1,0:T(8,128)} %param.9, s32[48]{0:T(128)S(1)} %and_select_fusion, s32[8,8]{1,0:T(8,128)} %param.8), kind=kLoop, calls=%fused_computation.7 | loop fusion | flops 8832 | bytes 2240 | tf_op jit(solution)/shard_map/reduce_sum | solution.py:173
  0.8 0.0 copy-start.3
  0.8 0.7 %copy-done.3 = bf16[8,2048]{1,0:T(8,128)(2,1)S(1)} copy-done((bf16[8,2048]{1,0:T(8,128)(2,1)S(1)}, bf16[8,2048]{1,0:T(8,128)(2,1)}, u32[]{:S(2)}) %copy-start.3) | copy-done | bytes 32792
  1.6 4.1 %collective-permute-start = (bf16[8,2176]{1,0:T(8,128)(2,1)S(1)}, bf16[8,2176]{1,0:T(8,128)(2,1)S(1)}, u32[]{:S(2)}, u32[]{:S(2)}) collective-permute-start(bf16[8,2176]{1,0:T(8,128)(2,1)S(1)} %shard_map.73.after), channel_id=1, source_target_pairs={{0,8},{1,9},{2,10},{3,11},{4,12},{5,13},{6,14},{7,15},{8,0},{9,1},... | collective-permute-start | bytes 104456 | tf_op jit(solution)/shard_map/ppermute | solution.py:73
  5.7 0.0 copy-start
  5.7 1.9 %copy-done = bf16[1,2048,768]{2,1,0:T(8,128)(2,1)S(1)} copy-done((bf16[1,2048,768]{2,1,0:T(8,128)(2,1)S(1)}, bf16[1,2048,768]{2,1,0:T(8,128)(2,1)}, u32[]{:S(2)}) %copy-start) | copy-done | bytes 3145752
  7.6 0.0 copy-start.1
  7.6 0.3 shard_map.74.refs_9_
  7.8 0.1 collective-permute-done
  8.0 0.0 copy-start.2
  8.0 2.5 %collective-permute-start.2 = (bf16[16,2176]{1,0:T(8,128)(2,1)S(1)}, bf16[16,2176]{1,0:T(8,128)(2,1)S(1)}, u32[]{:S(2)}, u32[]{:S(2)}) collective-permute-start(bf16[16,2176]{1,0:T(8,128)(2,1)S(1)} %pad_maximum_fusion.after.refs_0_), channel_id=1, source_target_pairs={{0,6},{1,7},{2,4},{3,5},{4,2},{5,3},{6,0},{7,1},{8,14},{9,15},{10,... | collective-permute-start | bytes 208904 | tf_op jit(solution)/shard_map/ppermute | solution.py:73
  10.5 0.5 %collective-permute-start.1 = (bf16[16,2176]{1,0:T(8,128)(2,1)S(1)}, bf16[16,2176]{1,0:T(8,128)(2,1)S(1)}, u32[]{:S(2)}, u32[]{:S(2)}) collective-permute-start(bf16[16,2176]{1,0:T(8,128)(2,1)S(1)} %pad_maximum_fusion.after.refs_0_), channel_id=1, source_target_pairs={{0,2},{1,3},{2,0},{3,1},{4,6},{5,7},{6,4},{7,5},{8,10},{9,11},{10,... | collective-permute-start | bytes 208904 | tf_op jit(solution)/shard_map/ppermute | solution.py:73
  11.0 0.0 collective-permute-start.4
  11.0 0.5 %collective-permute-start.3 = (bf16[16,2176]{1,0:T(8,128)(2,1)S(1)}, bf16[16,2176]{1,0:T(8,128)(2,1)S(1)}, u32[]{:S(2)}, u32[]{:S(2)}) collective-permute-start(bf16[16,2176]{1,0:T(8,128)(2,1)S(1)} %pad_maximum_fusion.after.refs_0_), channel_id=1, source_target_pairs={{0,4},{1,5},{2,6},{3,7},{4,0},{5,1},{6,2},{7,3},{8,12},{9,13},{10,... | collective-permute-start | bytes 208904 | tf_op jit(solution)/shard_map/ppermute | solution.py:73
  11.5 1.8 %collective-permute-done.2.refs_2_ = bf16[16,2176]{1,0:T(8,128)(2,1)S(1)} collective-permute-done((bf16[16,2176]{1,0:T(8,128)(2,1)S(1)}, bf16[16,2176]{1,0:T(8,128)(2,1)S(1)}, u32[]{:S(2)}, u32[]{:S(2)}) %collective-permute-start.2) | collective-permute-done | bytes 69664 | tf_op jit(solution)/shard_map/ppermute | solution.py:73
  13.4 0.0 collective-permute-start.5
  13.4 0.0 copy-done.1
  13.4 0.3 shard_map.76.refs_11_
  13.6 0.0 copy-done.2
  13.6 0.0 copy-start.4
  13.7 0.3 shard_map.75.refs_10_
  13.9 0.9 %collective-permute-done.1.refs_1_ = bf16[16,2176]{1,0:T(8,128)(2,1)S(1)} collective-permute-done((bf16[16,2176]{1,0:T(8,128)(2,1)S(1)}, bf16[16,2176]{1,0:T(8,128)(2,1)S(1)}, u32[]{:S(2)}, u32[]{:S(2)}) %collective-permute-start.1) | collective-permute-done | bytes 69664 | tf_op jit(solution)/shard_map/ppermute | solution.py:73
  14.8 0.0 collective-permute-start.6
  14.8 0.0 collective-permute-done.4.refs_5_
  14.8 0.8 %collective-permute-done.3.refs_3_ = bf16[16,2176]{1,0:T(8,128)(2,1)S(1)} collective-permute-done((bf16[16,2176]{1,0:T(8,128)(2,1)S(1)}, bf16[16,2176]{1,0:T(8,128)(2,1)S(1)}, u32[]{:S(2)}, u32[]{:S(2)}) %collective-permute-start.3) | collective-permute-done | bytes 69664 | tf_op jit(solution)/shard_map/ppermute | solution.py:73
  15.6 0.0 collective-permute-done.5.refs_6_
  15.6 0.0 collective-permute-start.7
  15.6 0.4 %collective-permute-done.6.refs_4_ = bf16[16,2176]{1,0:T(8,128)(2,1)S(1)} collective-permute-done((bf16[16,2176]{1,0:T(8,128)(2,1)S(1)}, bf16[16,2176]{1,0:T(8,128)(2,1)S(1)}, u32[]{:S(2)}, u32[]{:S(2)}) %collective-permute-start.6) | collective-permute-done | bytes 69664 | tf_op jit(solution)/shard_map/ppermute | solution.py:73
  16.1 0.8 %collective-permute-done.7.refs_7_ = bf16[16,2176]{1,0:T(8,128)(2,1)S(1)} collective-permute-done((bf16[16,2176]{1,0:T(8,128)(2,1)S(1)}, bf16[16,2176]{1,0:T(8,128)(2,1)S(1)}, u32[]{:S(2)}, u32[]{:S(2)}) %collective-permute-start.7) | collective-permute-done | bytes 69664 | tf_op jit(solution)/shard_map/ppermute | solution.py:73
  16.9 0.0 copy-done.4
  16.9 2.1 %shard_map.77 = (bf16[16,2048]{1,0:T(8,128)(2,1)S(1)}, bf16[16,2048]{1,0:T(8,128)(2,1)S(1)}, bf16[16,2048]{1,0:T(8,128)(2,1)S(1)}, bf16[16,2048]{1,0:T(8,128)(2,...) custom-call(bf16[16,2176]{1,0:T(8,128)(2,1)S(1)} %pad_maximum_fusion.after.refs_0_, ...), custom_call_target="tpu_custom_call" | custom-call | tf_op jit(solution)/shard_map/pallas_call | solution.py:196
  19.0 0.2 collective-permute-start.9
  19.2 0.4 %collective-permute-start.8 = (bf16[48,2048]{1,0:T(8,128)(2,1)S(1)}, bf16[48,2048]{1,0:T(8,128)(2,1)S(1)}, u32[]{:S(2)}, u32[]{:S(2)}) collective-permute-start(bf16[48,2048]{1,0:T(8,128)(2,1)S(1)} %get-tuple-element.26), channel_id=1, source_target_pairs={{0,1},{1,0},{2,3},{3,2},{4,5},{5,4},{6,7},{7,6},{8,9},{9,8},{10,11... | collective-permute-start | bytes 589832 | tf_op jit(solution)/shard_map/ppermute | solution.py:73
  19.6 0.7 %collective-permute-done.9 = bf16[16,2048]{1,0:T(8,128)(2,1)S(1)} collective-permute-done((bf16[16,2048]{1,0:T(8,128)(2,1)S(1)}, bf16[16,2048]{1,0:T(8,128)(2,1)S(1)}, u32[]{:S(2)}, u32[]{:S(2)}) %collective-permute-start.9) | collective-permute-done | bytes 65568 | tf_op jit(solution)/shard_map/ppermute | solution.py:73
  20.3 1.6 %collective-permute-start.10 = (bf16[16,2048]{1,0:T(8,128)(2,1)S(1)}, bf16[16,2048]{1,0:T(8,128)(2,1)S(1)}, u32[]{:S(2)}, u32[]{:S(2)}) collective-permute-start(bf16[16,2048]{1,0:T(8,128)(2,1)S(1)} %add_convert_fusion.2), channel_id=1, source_target_pairs={{0,2},{1,3},{2,0},{3,1},{4,6},{5,7},{6,4},{7,5},{8,10},{9,11},{10,... | collective-permute-start | bytes 196616 | tf_op jit(solution)/shard_map/ppermute | solution.py:73
  21.9 0.0 collective-permute-done.8
  21.9 0.7 %collective-permute-start.11 = (bf16[16,2048]{1,0:T(8,128)(2,1)S(1)}, bf16[16,2048]{1,0:T(8,128)(2,1)S(1)}, u32[]{:S(2)}, u32[]{:S(2)}) collective-permute-start(bf16[16,2048]{1,0:T(8,128)(2,1)S(1)} %get-tuple-element.33), channel_id=1, source_target_pairs={{0,6},{1,7},{2,4},{3,5},{4,2},{5,3},{6,0},{7,1},{8,14},{9,15},{10,... | collective-permute-start | bytes 196616 | tf_op jit(solution)/shard_map/ppermute | solution.py:73
  22.6 1.4 %collective-permute-start.12 = (bf16[16,2048]{1,0:T(8,128)(2,1)S(1)}, bf16[16,2048]{1,0:T(8,128)(2,1)S(1)}, u32[]{:S(2)}, u32[]{:S(2)}) collective-permute-start(bf16[16,2048]{1,0:T(8,128)(2,1)S(1)} %get-tuple-element.32), channel_id=1, source_target_pairs={{0,4},{1,5},{2,6},{3,7},{4,0},{5,1},{6,2},{7,3},{8,12},{9,13},{10,... | collective-permute-start | bytes 196616 | tf_op jit(solution)/shard_map/ppermute | solution.py:73
  24.0 0.7 %collective-permute-done.10 = bf16[16,2048]{1,0:T(8,128)(2,1)S(1)} collective-permute-done((bf16[16,2048]{1,0:T(8,128)(2,1)S(1)}, bf16[16,2048]{1,0:T(8,128)(2,1)S(1)}, u32[]{:S(2)}, u32[]{:S(2)}) %collective-permute-start.10) | collective-permute-done | bytes 65568 | tf_op jit(solution)/shard_map/ppermute | solution.py:73
  24.6 2.8 %collective-permute-done.11 = bf16[16,2048]{1,0:T(8,128)(2,1)S(1)} collective-permute-done((bf16[16,2048]{1,0:T(8,128)(2,1)S(1)}, bf16[16,2048]{1,0:T(8,128)(2,1)S(1)}, u32[]{:S(2)}, u32[]{:S(2)}) %collective-permute-start.11) | collective-permute-done | bytes 65568 | tf_op jit(solution)/shard_map/ppermute | solution.py:73
  27.5 0.0 collective-permute-done.12
  27.5 2.9 %collective-permute-start.13 = (bf16[8,2048]{1,0:T(8,128)(2,1)S(1)}, bf16[8,2048]{1,0:T(8,128)(2,1)S(1)}, u32[]{:S(2)}, u32[]{:S(2)}) collective-permute-start(bf16[8,2048]{1,0:T(8,128)(2,1)S(1)} %add_convert_fusion.5), channel_id=1, source_target_pairs={{0,8},{1,9},{2,10},{3,11},{4,12},{5,13},{6,14},{7,15},{8,0},{9,1},... | collective-permute-start | bytes 98312 | tf_op jit(solution)/shard_map/ppermute | solution.py:73
  30.4 2.0 %collective-permute-done.13 = bf16[8,2048]{1,0:T(8,128)(2,1)S(1)} collective-permute-done((bf16[8,2048]{1,0:T(8,128)(2,1)S(1)}, bf16[8,2048]{1,0:T(8,128)(2,1)S(1)}, u32[]{:S(2)}, u32[]{:S(2)}) %collective-permute-start.13) | collective-permute-done | bytes 32800 | tf_op jit(solution)/shard_map/ppermute | solution.py:73
  32.4 0.6 %add_convert_fusion.4 = bf16[8,2048]{1,0:T(8,128)(2,1)} fusion(bf16[8,2048]{1,0:T(8,128)(2,1)S(1)} %collective-permute-done.13, bf16[16,2048]{1,0:T(8,128)(2,1)S(1)} %collective-permute-done.12, bf16[16,2048]{1,0:T(8,128)(2,1)S(1)} %collective-permute-done.11, bf16[16,2048]{1,0:T(8,128)(2,1)S(1)} %collective-permute-done.10, ...), kind=kLoop, calls=%fused_computation.5 | loop fusion | flops 163840 | bytes 196608 | tf_op jit(solution)/shard_map/convert_element_type | solution.py:85
  (6 shorter events, 0.1 us)
Async XLA Ops:
  0.8 0.8 %copy-start.3 = (bf16[8,2048]{1,0:T(8,128)(2,1)S(1)}, bf16[8,2048]{1,0:T(8,128)(2,1)}, u32[]{:S(2)}) copy-start(bf16[8,2048]{1,0:T(8,128)(2,1)} %tokens_ref.1) | copy-start | bytes 98308
  1.6 6.4 %collective-permute-start = (bf16[8,2176]{1,0:T(8,128)(2,1)S(1)}, bf16[8,2176]{1,0:T(8,128)(2,1)S(1)}, u32[]{:S(2)}, u32[]{:S(2)}) collective-permute-start(bf16[8,2176]{1,0:T(8,128)(2,1)S(1)} %shard_map.73.after), channel_id=1, source_target_pairs={{0,8},{1,9},{2,10},{3,11},{4,12},{5,13},{6,14},{7,15},{8,0},{9,1},... | collective-permute-start | bytes 104456 | tf_op jit(solution)/shard_map/ppermute | solution.py:73
  5.7 1.9 %copy-start = (bf16[1,2048,768]{2,1,0:T(8,128)(2,1)S(1)}, bf16[1,2048,768]{2,1,0:T(8,128)(2,1)}, u32[]{:S(2)}) copy-start(bf16[1,2048,768]{2,1,0:T(8,128)(2,1)} %source.3) | copy-start | bytes 9437188
  7.6 5.8 %copy-start.1 = (bf16[1,768,2048]{2,1,0:T(8,128)(2,1)S(1)}, bf16[1,768,2048]{2,1,0:T(8,128)(2,1)}, u32[]{:S(2)}) copy-start(bf16[1,768,2048]{2,1,0:T(8,128)(2,1)} %source.5) | copy-start | bytes 9437188
  8.0 5.7 %copy-start.2 = (bf16[1,2048,768]{2,1,0:T(8,128)(2,1)S(1)}, bf16[1,2048,768]{2,1,0:T(8,128)(2,1)}, u32[]{:S(2)}) copy-start(bf16[1,2048,768]{2,1,0:T(8,128)(2,1)} %source.4) | copy-start | bytes 9437188
  8.0 5.4 %collective-permute-start.2 = (bf16[16,2176]{1,0:T(8,128)(2,1)S(1)}, bf16[16,2176]{1,0:T(8,128)(2,1)S(1)}, u32[]{:S(2)}, u32[]{:S(2)}) collective-permute-start(bf16[16,2176]{1,0:T(8,128)(2,1)S(1)} %pad_maximum_fusion.after.refs_0_), channel_id=1, source_target_pairs={{0,6},{1,7},{2,4},{3,5},{4,2},{5,3},{6,0},{7,1},{8,14},{9,15},{10,... | collective-permute-start | bytes 208904 | tf_op jit(solution)/shard_map/ppermute | solution.py:73
  10.5 4.3 %collective-permute-start.1 = (bf16[16,2176]{1,0:T(8,128)(2,1)S(1)}, bf16[16,2176]{1,0:T(8,128)(2,1)S(1)}, u32[]{:S(2)}, u32[]{:S(2)}) collective-permute-start(bf16[16,2176]{1,0:T(8,128)(2,1)S(1)} %pad_maximum_fusion.after.refs_0_), channel_id=1, source_target_pairs={{0,2},{1,3},{2,0},{3,1},{4,6},{5,7},{6,4},{7,5},{8,10},{9,11},{10,... | collective-permute-start | bytes 208904 | tf_op jit(solution)/shard_map/ppermute | solution.py:73
  11.0 3.8 %collective-permute-start.4 = (bf16[16,2176]{1,0:T(8,128)(2,1)S(1)}, bf16[16,2176]{1,0:T(8,128)(2,1)S(1)}, u32[]{:S(2)}, u32[]{:S(2)}) collective-permute-start(bf16[16,2176]{1,0:T(8,128)(2,1)S(1)} %pad_maximum_fusion.after.refs_0_), channel_id=1, source_target_pairs={{0,1},{1,0},{2,3},{3,2},{4,5},{5,4},{6,7},{7,6},{8,9},{9,8},{10,11... | collective-permute-start | bytes 208904 | tf_op jit(solution)/shard_map/ppermute | solution.py:73
  11.0 4.6 %collective-permute-start.3 = (bf16[16,2176]{1,0:T(8,128)(2,1)S(1)}, bf16[16,2176]{1,0:T(8,128)(2,1)S(1)}, u32[]{:S(2)}, u32[]{:S(2)}) collective-permute-start(bf16[16,2176]{1,0:T(8,128)(2,1)S(1)} %pad_maximum_fusion.after.refs_0_), channel_id=1, source_target_pairs={{0,4},{1,5},{2,6},{3,7},{4,0},{5,1},{6,2},{7,3},{8,12},{9,13},{10,... | collective-permute-start | bytes 208904 | tf_op jit(solution)/shard_map/ppermute | solution.py:73
  13.4 2.3 %collective-permute-start.5 = (bf16[16,2176]{1,0:T(8,128)(2,1)S(1)}, bf16[16,2176]{1,0:T(8,128)(2,1)S(1)}, u32[]{:S(2)}, u32[]{:S(2)}) collective-permute-start(bf16[16,2176]{1,0:T(8,128)(2,1)S(1)} %collective-permute-done.2.refs_2_), channel_id=1, source_target_pairs={{0,1},{1,0},{2,3},{3,2},{4,5},{5,4},{6,7},{7,6},{8,9},{9,8},{10,11... | collective-permute-start | bytes 208904 | tf_op jit(solution)/shard_map/ppermute | solution.py:73
  13.6 3.3 %copy-start.4 = (s32[1,6]{1,0:T(1,128)S(1)}, s32[1,6]{1,0:T(1,128)}, u32[]{:S(2)}) copy-start(s32[1,6]{1,0:T(1,128)} %refs_8_.1) | copy-start | bytes 76
  14.8 1.3 %collective-permute-start.6 = (bf16[16,2176]{1,0:T(8,128)(2,1)S(1)}, bf16[16,2176]{1,0:T(8,128)(2,1)S(1)}, u32[]{:S(2)}, u32[]{:S(2)}) collective-permute-start(bf16[16,2176]{1,0:T(8,128)(2,1)S(1)} %collective-permute-done.1.refs_1_), channel_id=1, source_target_pairs={{0,1},{1,0},{2,3},{3,2},{4,5},{5,4},{6,7},{7,6},{8,9},{9,8},{10,11... | collective-permute-start | bytes 208904 | tf_op jit(solution)/shard_map/ppermute | solution.py:73
  15.6 1.3 %collective-permute-start.7 = (bf16[16,2176]{1,0:T(8,128)(2,1)S(1)}, bf16[16,2176]{1,0:T(8,128)(2,1)S(1)}, u32[]{:S(2)}, u32[]{:S(2)}) collective-permute-start(bf16[16,2176]{1,0:T(8,128)(2,1)S(1)} %collective-permute-done.3.refs_3_), channel_id=1, source_target_pairs={{0,1},{1,0},{2,3},{3,2},{4,5},{5,4},{6,7},{7,6},{8,9},{9,8},{10,11... | collective-permute-start | bytes 208904 | tf_op jit(solution)/shard_map/ppermute | solution.py:73
  19.0 1.3 %collective-permute-start.9 = (bf16[16,2048]{1,0:T(8,128)(2,1)S(1)}, bf16[16,2048]{1,0:T(8,128)(2,1)S(1)}, u32[]{:S(2)}, u32[]{:S(2)}) collective-permute-start(bf16[16,2048]{1,0:T(8,128)(2,1)S(1)} %get-tuple-element.28), channel_id=1, source_target_pairs={{0,1},{1,0},{2,3},{3,2},{4,5},{5,4},{6,7},{7,6},{8,9},{9,8},{10,11... | collective-permute-start | bytes 196616 | tf_op jit(solution)/shard_map/ppermute | solution.py:73
  19.2 2.7 %collective-permute-start.8 = (bf16[48,2048]{1,0:T(8,128)(2,1)S(1)}, bf16[48,2048]{1,0:T(8,128)(2,1)S(1)}, u32[]{:S(2)}, u32[]{:S(2)}) collective-permute-start(bf16[48,2048]{1,0:T(8,128)(2,1)S(1)} %get-tuple-element.26), channel_id=1, source_target_pairs={{0,1},{1,0},{2,3},{3,2},{4,5},{5,4},{6,7},{7,6},{8,9},{9,8},{10,11... | collective-permute-start | bytes 589832 | tf_op jit(solution)/shard_map/ppermute | solution.py:73
  20.3 4.3 %collective-permute-start.10 = (bf16[16,2048]{1,0:T(8,128)(2,1)S(1)}, bf16[16,2048]{1,0:T(8,128)(2,1)S(1)}, u32[]{:S(2)}, u32[]{:S(2)}) collective-permute-start(bf16[16,2048]{1,0:T(8,128)(2,1)S(1)} %add_convert_fusion.2), channel_id=1, source_target_pairs={{0,2},{1,3},{2,0},{3,1},{4,6},{5,7},{6,4},{7,5},{8,10},{9,11},{10,... | collective-permute-start | bytes 196616 | tf_op jit(solution)/shard_map/ppermute | solution.py:73
  21.9 5.5 %collective-permute-start.11 = (bf16[16,2048]{1,0:T(8,128)(2,1)S(1)}, bf16[16,2048]{1,0:T(8,128)(2,1)S(1)}, u32[]{:S(2)}, u32[]{:S(2)}) collective-permute-start(bf16[16,2048]{1,0:T(8,128)(2,1)S(1)} %get-tuple-element.33), channel_id=1, source_target_pairs={{0,6},{1,7},{2,4},{3,5},{4,2},{5,3},{6,0},{7,1},{8,14},{9,15},{10,... | collective-permute-start | bytes 196616 | tf_op jit(solution)/shard_map/ppermute | solution.py:73
  22.6 4.8 %collective-permute-start.12 = (bf16[16,2048]{1,0:T(8,128)(2,1)S(1)}, bf16[16,2048]{1,0:T(8,128)(2,1)S(1)}, u32[]{:S(2)}, u32[]{:S(2)}) collective-permute-start(bf16[16,2048]{1,0:T(8,128)(2,1)S(1)} %get-tuple-element.32), channel_id=1, source_target_pairs={{0,4},{1,5},{2,6},{3,7},{4,0},{5,1},{6,2},{7,3},{8,12},{9,13},{10,... | collective-permute-start | bytes 196616 | tf_op jit(solution)/shard_map/ppermute | solution.py:73
  27.5 4.9 %collective-permute-start.13 = (bf16[8,2048]{1,0:T(8,128)(2,1)S(1)}, bf16[8,2048]{1,0:T(8,128)(2,1)S(1)}, u32[]{:S(2)}, u32[]{:S(2)}) collective-permute-start(bf16[8,2048]{1,0:T(8,128)(2,1)S(1)} %add_convert_fusion.5), channel_id=1, source_target_pairs={{0,8},{1,9},{2,10},{3,11},{4,12},{5,13},{6,14},{7,15},{8,0},{9,1},... | collective-permute-start | bytes 98312 | tf_op jit(solution)/shard_map/ppermute | solution.py:73

commit v6 on v5

--- a/solution.py
+++ b/solution.py
@@ -126,7 +126,11 @@
 
 
 def expert_kernel(experts, n_pieces, *refs):
-    pieces = refs[:n_pieces]
+    own, four, six, two, own_far, four_far, six_far, two_far = (piece[...] for piece in refs[:n_pieces])
+    second = lax.axis_index("expert") % 2 == 1
+    duty = [jnp.where(second, six, four), jnp.where(second, six_far, four_far)]
+    given = [jnp.where(second, four_far, six_far), jnp.where(second, four, six)]
+    pieces = [own, two, *duty, own_far, *given, two_far]
     mask_ref, gate_ref, up_ref, down_ref = refs[n_pieces : n_pieces + 4]
     *answers, rows, hidden = refs[n_pieces + 4 :]
     width, units = gate_ref.shape[1:]
@@ -179,7 +183,7 @@
         compiler_params=pltpu.CompilerParams(vmem_limit_bytes=1 << 20),
     )(tokens, shares)
     own, gate_here = joined(packed, swap(packed, 8, experts), load(gate_weight, packed))
-    order = (4, 2, 6)
+    order = (4, 6, 2)
     arrived = {distance: swap(own, distance, experts) for distance in order}
     own_far = swap(own, 1, experts)
     last, first = order[0], order[2]
@@ -189,11 +193,11 @@
     )
     far = {distance: swap(arrived[distance], 1, experts) for distance in order[:2]}
     far[first] = first_far
-    pieces = [own, *[arrived[d] for d in (2, 6, 4)], far[(2, 6, 4)[0]], own_far, *[far[d] for d in (2, 6, 4)[1:]]]
+    pieces = [own, arrived[2], arrived[4], arrived[6], own_far, far[2], far[4], far[6]]
     total = sum(piece.shape[0] for piece in pieces)
     block = own.shape[0]
-    heights = [block] * 5 + [3 * block]
-    *mine, first_far, rest_far = pl.pallas_call(
+    heights = [block, block, 2 * block, block, 2 * block, block]
+    own, two, duty, own_far, given, two_far = pl.pallas_call(
         functools.partial(expert_kernel, experts, len(pieces)),
         out_shape=[jax.ShapeDtypeStruct((height, model_width), jnp.bfloat16) for height in heights],
         in_specs=[WHOLE] * len(pieces) + [pl.BlockSpec(memory_space=pltpu.SMEM)] + [WHOLE] * 3,
@@ -201,11 +205,11 @@
         scratch_shapes=[pltpu.VMEM((total, model_width), jnp.bfloat16), pltpu.VMEM((total, units), jnp.bfloat16)],
         compiler_params=pltpu.CompilerParams(vmem_limit_bytes=16 << 20),
     )(*pieces, prune_mask, gate_here, up_here, down_here)
-    first_far, rest_far = swap(first_far, 1, experts), swap(rest_far, 1, experts)
-    others = [rest_far[:block], first_far, rest_far[block : 2 * block], rest_far[2 * block :]]
-    sums = [add(here, there) for here, there in zip(mine, others)]
-    sums = sums[:1] + [lax.optimization_barrier(one) for one in sums[1:]]
-    terms = sums[:1] + [swap(one, distance, experts) for one, distance in zip(sums[1:], (2, 6, 4))]
+    duty = lax.optimization_barrier(add(duty, swap(given, 1, experts)))
+    two = lax.optimization_barrier(add(two, swap(two_far, 1, experts)))
+    duty, two = swap_apart(duty, 2, 4, experts), swap(two, 6, experts)
+    own_far = swap(lax.optimization_barrier(add(own_far, duty[block:])), 1, experts)
+    terms = [own, duty[:block], two, own_far]
     sent = lax.optimization_barrier(add(*[term[tok_dev:] for term in terms]))
     return add(*[term[:tok_dev] for term in terms], swap(sent, 8, experts))
 

time: 33.3 us -> 33 us (level)
  starting transfers between devices: 14.8 us -> 14.2 us
  waiting for transfers between devices: 11.1 us -> 11.5 us
    ppermute x0 -> x1, waiting for transfers between devices: none -> 2.48 us  [swap_apart(): lax.ppermute(block, 'expert', [(i, i ^ (odd if i % 2 else even)) for i in...]
    ppermute x14 -> x13, waiting for transfers between devices: 11.1 us -> 8.97 us  [swap(): lax.ppermute(block, 'expert', [(i, i ^ distance) for i in range(experts)])]
    ppermute x14 -> x13, starting transfers between devices: 14.8 us -> 12.7 us  [swap(): lax.ppermute(block, 'expert', [(i, i ^ distance) for i in range(experts)])]
    ppermute x0 -> x1, starting transfers between devices: none -> 1.55 us  [swap_apart(): lax.ppermute(block, 'expert', [(i, i ^ (odd if i % 2 else even)) for i in...]
    convert_element_type x4 -> x5, other arithmetic: 0.73 us -> 0.73 us  [add(): functools.reduce(jnp.add, [block.astype(jnp.float32) for block in blocks])]
where the time goes in v6:
time: 33 us; the launch traced here: 32.8 us
  starting transfers between devices  14.2 us (43%)
  waiting for transfers between devices  11.5 us (35%)
  Pallas kernels  2.85 us (9%)
  local copies, waits for them, and re-layouts  2.66 us (8%)
  other arithmetic  1.53 us (5%)
    ppermute x13, starting transfers between devices, swap(): lax.ppermute(block, 'expert', [(i, i ^ distance) for i in range(experts)])  12.7 us
    ppermute x13, waiting for transfers between devices, swap(): lax.ppermute(block, 'expert', [(i, i ^ distance) for i in range(experts)])  8.97 us
    unnamed x10, local copies, waits for them, and re-layouts  2.66 us
    ppermute x1, waiting for transfers between devices, swap_apart(): lax.ppermute(block, 'expert', [(i, i ^ (odd if i % 2 else even)) for i in...  2.48 us
    pallas_call x1, Pallas kernels, dense_body(): pl.pallas_call(functools.partial(expert_kernel, experts, len(pieces)), ou...  2.08 us
    ppermute x1, starting transfers between devices, swap_apart(): lax.ppermute(block, 'expert', [(i, i ^ (odd if i % 2 else even)) for i in...  1.55 us
    reduce_sum x1, other arithmetic, dense_body(): shares = jnp.sum(jnp.where(chosen, combine[:, :, None], 0.0), axis=1)  0.79 us
    pallas_call x3, Pallas kernels, load(): pl.pallas_call(load_kernel, out_shape=jax.ShapeDtypeStruct(source.shape,...  0.76 us
  transfers between devices with their start and end apart: 14, of which 10 were waited for; matrix products, arithmetic and copies ran while one was open for 0% of the time, Pallas kernels for 2%

profile of v6, /device:TPU:0, one launch (start us, length us, event | category | flops | bytes accessed | tf_op | source)
XLA Modules:
  0.0 32.8 jit_solution(9581446936320608480)
XLA Ops:
  0.0 0.8 %select_reduce_fusion.share_ref = f32[8,48]{1,0:T(8,128)S(1)} fusion(f32[8,8]{1,0:T(8,128)} %param.9, s32[48]{0:T(128)S(1)} %and_select_fusion, s32[8,8]{1,0:T(8,128)} %param.8), kind=kLoop, calls=%fused_computation.6 | loop fusion | flops 8832 | bytes 2240 | tf_op jit(solution)/shard_map/reduce_sum | solution.py:177
  0.8 0.0 copy-start.3
  0.8 0.7 %copy-done.3 = bf16[8,2048]{1,0:T(8,128)(2,1)S(1)} copy-done((bf16[8,2048]{1,0:T(8,128)(2,1)S(1)}, bf16[8,2048]{1,0:T(8,128)(2,1)}, u32[]{:S(2)}) %copy-start.3) | copy-done | bytes 32792
  1.6 4.1 %collective-permute-start = (bf16[8,2176]{1,0:T(8,128)(2,1)S(1)}, bf16[8,2176]{1,0:T(8,128)(2,1)S(1)}, u32[]{:S(2)}, u32[]{:S(2)}) collective-permute-start(bf16[8,2176]{1,0:T(8,128)(2,1)S(1)} %shard_map.73.after), channel_id=1, source_target_pairs={{0,8},{1,9},{2,10},{3,11},{4,12},{5,13},{6,14},{7,15},{8,0},{9,1},... | collective-permute-start | bytes 104456 | tf_op jit(solution)/shard_map/ppermute | solution.py:73
  5.7 0.0 copy-start
  5.7 1.9 %copy-done = bf16[1,2048,768]{2,1,0:T(8,128)(2,1)S(1)} copy-done((bf16[1,2048,768]{2,1,0:T(8,128)(2,1)S(1)}, bf16[1,2048,768]{2,1,0:T(8,128)(2,1)}, u32[]{:S(2)}) %copy-start) | copy-done | bytes 3145752
  7.6 0.0 copy-start.1
  7.6 0.3 shard_map.74.refs_9_
  7.8 0.1 collective-permute-done
  8.0 0.0 copy-start.2
  8.0 1.8 %collective-permute-start.1 = (bf16[16,2176]{1,0:T(8,128)(2,1)S(1)}, bf16[16,2176]{1,0:T(8,128)(2,1)S(1)}, u32[]{:S(2)}, u32[]{:S(2)}) collective-permute-start(bf16[16,2176]{1,0:T(8,128)(2,1)S(1)} %pad_maximum_fusion.after.refs_0_), channel_id=1, source_target_pairs={{0,2},{1,3},{2,0},{3,1},{4,6},{5,7},{6,4},{7,5},{8,10},{9,11},{10,... | collective-permute-start | bytes 208904 | tf_op jit(solution)/shard_map/ppermute | solution.py:73
  9.7 1.3 %collective-permute-start.5 = (bf16[16,2176]{1,0:T(8,128)(2,1)S(1)}, bf16[16,2176]{1,0:T(8,128)(2,1)S(1)}, u32[]{:S(2)}, u32[]{:S(2)}) collective-permute-start(bf16[16,2176]{1,0:T(8,128)(2,1)S(1)} %pad_maximum_fusion.after.refs_0_), channel_id=1, source_target_pairs={{0,6},{1,7},{2,4},{3,5},{4,2},{5,3},{6,0},{7,1},{8,14},{9,15},{10,... | collective-permute-start | bytes 208904 | tf_op jit(solution)/shard_map/ppermute | solution.py:73
  11.0 0.0 collective-permute-start.3
  11.0 0.5 %collective-permute-start.2 = (bf16[16,2176]{1,0:T(8,128)(2,1)S(1)}, bf16[16,2176]{1,0:T(8,128)(2,1)S(1)}, u32[]{:S(2)}, u32[]{:S(2)}) collective-permute-start(bf16[16,2176]{1,0:T(8,128)(2,1)S(1)} %pad_maximum_fusion.after.refs_0_), channel_id=1, source_target_pairs={{0,4},{1,5},{2,6},{3,7},{4,0},{5,1},{6,2},{7,3},{8,12},{9,13},{10,... | collective-permute-start | bytes 208904 | tf_op jit(solution)/shard_map/ppermute | solution.py:73
  11.5 1.6 %collective-permute-done.1.refs_1_ = bf16[16,2176]{1,0:T(8,128)(2,1)S(1)} collective-permute-done((bf16[16,2176]{1,0:T(8,128)(2,1)S(1)}, bf16[16,2176]{1,0:T(8,128)(2,1)S(1)}, u32[]{:S(2)}, u32[]{:S(2)}) %collective-permute-start.1) | collective-permute-done | bytes 69664 | tf_op jit(solution)/shard_map/ppermute | solution.py:73
  13.1 0.0 collective-permute-start.4
  13.1 0.0 copy-done.1
  13.1 0.3 shard_map.76.refs_11_
  13.4 0.0 copy-done.2
  13.4 0.0 copy-start.4
  13.4 0.3 shard_map.75.refs_10_
  13.7 1.3 %collective-permute-done.5.refs_3_ = bf16[16,2176]{1,0:T(8,128)(2,1)S(1)} collective-permute-done((bf16[16,2176]{1,0:T(8,128)(2,1)S(1)}, bf16[16,2176]{1,0:T(8,128)(2,1)S(1)}, u32[]{:S(2)}, u32[]{:S(2)}) %collective-permute-start.5) | collective-permute-done | bytes 69664 | tf_op jit(solution)/shard_map/ppermute | solution.py:73
  15.0 0.0 collective-permute-start.7
  15.0 0.0 collective-permute-done.3.refs_4_
  15.0 0.7 %collective-permute-done.2.refs_2_ = bf16[16,2176]{1,0:T(8,128)(2,1)S(1)} collective-permute-done((bf16[16,2176]{1,0:T(8,128)(2,1)S(1)}, bf16[16,2176]{1,0:T(8,128)(2,1)S(1)}, u32[]{:S(2)}, u32[]{:S(2)}) %collective-permute-start.2) | collective-permute-done | bytes 69664 | tf_op jit(solution)/shard_map/ppermute | solution.py:73
  15.6 0.0 collective-permute-done.4.refs_5_
  15.6 0.0 collective-permute-start.6
  15.6 0.6 %collective-permute-done.7.refs_7_ = bf16[16,2176]{1,0:T(8,128)(2,1)S(1)} collective-permute-done((bf16[16,2176]{1,0:T(8,128)(2,1)S(1)}, bf16[16,2176]{1,0:T(8,128)(2,1)S(1)}, u32[]{:S(2)}, u32[]{:S(2)}) %collective-permute-start.7) | collective-permute-done | bytes 69664 | tf_op jit(solution)/shard_map/ppermute | solution.py:73
  16.2 0.7 %collective-permute-done.6.refs_6_ = bf16[16,2176]{1,0:T(8,128)(2,1)S(1)} collective-permute-done((bf16[16,2176]{1,0:T(8,128)(2,1)S(1)}, bf16[16,2176]{1,0:T(8,128)(2,1)S(1)}, u32[]{:S(2)}, u32[]{:S(2)}) %collective-permute-start.6) | collective-permute-done | bytes 69664 | tf_op jit(solution)/shard_map/ppermute | solution.py:73
  16.9 0.0 copy-done.4
  16.9 2.1 %shard_map.77 = (bf16[16,2048]{1,0:T(8,128)(2,1)S(1)}, bf16[16,2048]{1,0:T(8,128)(2,1)S(1)}, bf16[32,2048]{1,0:T(8,128)(2,1)S(1)}, bf16[16,2048]{1,0:T(8,128)(2,...) custom-call(bf16[16,2176]{1,0:T(8,128)(2,1)S(1)} %pad_maximum_fusion.after.refs_0_, ...), custom_call_target="tpu_custom_call" | custom-call | tf_op jit(solution)/shard_map/pallas_call | solution.py:200
  19.0 0.2 collective-permute-start.8
  19.2 0.4 %collective-permute-start.10 = (bf16[16,2048]{1,0:T(8,128)(2,1)S(1)}, bf16[16,2048]{1,0:T(8,128)(2,1)S(1)}, u32[]{:S(2)}, u32[]{:S(2)}) collective-permute-start(bf16[16,2048]{1,0:T(8,128)(2,1)S(1)} %get-tuple-element.29), channel_id=1, source_target_pairs={{0,1},{1,0},{2,3},{3,2},{4,5},{5,4},{6,7},{7,6},{8,9},{9,8},{10,11... | collective-permute-start | bytes 196616 | tf_op jit(solution)/shard_map/ppermute | solution.py:73
  19.6 0.8 %collective-permute-done.8 = bf16[32,2048]{1,0:T(8,128)(2,1)S(1)} collective-permute-done((bf16[32,2048]{1,0:T(8,128)(2,1)S(1)}, bf16[32,2048]{1,0:T(8,128)(2,1)S(1)}, u32[]{:S(2)}, u32[]{:S(2)}) %collective-permute-start.8) | collective-permute-done | bytes 131104 | tf_op jit(solution)/shard_map/ppermute | solution.py:73
  20.4 1.5 %collective-permute-start.9 = (bf16[32,2048]{1,0:T(8,128)(2,1)S(1)}, bf16[32,2048]{1,0:T(8,128)(2,1)S(1)}, u32[]{:S(2)}, u32[]{:S(2)}) collective-permute-start(bf16[32,2048]{1,0:T(8,128)(2,1)S(1)} %add_convert_fusion), channel_id=1, source_target_pairs={{0,2},{1,5},{2,0},{3,7},{4,6},{5,1},{6,4},{7,3},{8,10},{9,13},{10,... | collective-permute-start | bytes 393224 | tf_op jit(solution)/shard_map/ppermute | solution.py:77
  22.0 0.0 collective-permute-done.10
  22.0 1.4 %collective-permute-start.11 = (bf16[16,2048]{1,0:T(8,128)(2,1)S(1)}, bf16[16,2048]{1,0:T(8,128)(2,1)S(1)}, u32[]{:S(2)}, u32[]{:S(2)}) collective-permute-start(bf16[16,2048]{1,0:T(8,128)(2,1)S(1)} %add_convert_fusion.2), channel_id=1, source_target_pairs={{0,6},{1,7},{2,4},{3,5},{4,2},{5,3},{6,0},{7,1},{8,14},{9,15},{10,... | collective-permute-start | bytes 196616 | tf_op jit(solution)/shard_map/ppermute | solution.py:73
  23.4 2.5 %collective-permute-done.9 = bf16[32,2048]{1,0:T(8,128)(2,1)S(1)} collective-permute-done((bf16[32,2048]{1,0:T(8,128)(2,1)S(1)}, bf16[32,2048]{1,0:T(8,128)(2,1)S(1)}, u32[]{:S(2)}, u32[]{:S(2)}) %collective-permute-start.9) | collective-permute-done | bytes 131104 | tf_op jit(solution)/shard_map/ppermute | solution.py:77
  25.9 0.1 collective-permute-start.12
  26.0 1.2 %collective-permute-done.11 = bf16[16,2048]{1,0:T(8,128)(2,1)S(1)} collective-permute-done((bf16[16,2048]{1,0:T(8,128)(2,1)S(1)}, bf16[16,2048]{1,0:T(8,128)(2,1)S(1)}, u32[]{:S(2)}, u32[]{:S(2)}) %collective-permute-start.11) | collective-permute-done | bytes 65568 | tf_op jit(solution)/shard_map/ppermute | solution.py:73
  27.2 0.0 collective-permute-done.12
  27.3 2.9 %collective-permute-start.13 = (bf16[8,2048]{1,0:T(8,128)(2,1)S(1)}, bf16[8,2048]{1,0:T(8,128)(2,1)S(1)}, u32[]{:S(2)}, u32[]{:S(2)}) collective-permute-start(bf16[8,2048]{1,0:T(8,128)(2,1)S(1)} %add_convert_fusion.4), channel_id=1, source_target_pairs={{0,8},{1,9},{2,10},{3,11},{4,12},{5,13},{6,14},{7,15},{8,0},{9,1},... | collective-permute-start | bytes 98312 | tf_op jit(solution)/shard_map/ppermute | solution.py:73
  30.2 2.0 %collective-permute-done.13 = bf16[8,2048]{1,0:T(8,128)(2,1)S(1)} collective-permute-done((bf16[8,2048]{1,0:T(8,128)(2,1)S(1)}, bf16[8,2048]{1,0:T(8,128)(2,1)S(1)}, u32[]{:S(2)}, u32[]{:S(2)}) %collective-permute-start.13) | collective-permute-done | bytes 32800 | tf_op jit(solution)/shard_map/ppermute | solution.py:73
  32.2 0.6 %add_convert_fusion.3 = bf16[8,2048]{1,0:T(8,128)(2,1)} fusion(bf16[8,2048]{1,0:T(8,128)(2,1)S(1)} %collective-permute-done.13, bf16[16,2048]{1,0:T(8,128)(2,1)S(1)} %collective-permute-done.12, bf16[16,2048]{1,0:T(8,128)(2,1)S(1)} %collective-permute-done.11, bf16[32,2048]{1,0:T(8,128)(2,1)S(1)} %collective-permute-done.9, ...), kind=kLoop, calls=%fused_computation.4 | loop fusion | flops 163840 | bytes 196608 | tf_op jit(solution)/shard_map/convert_element_type | solution.py:85
  (7 shorter events, 0.1 us)
Async XLA Ops:
  0.8 0.8 %copy-start.3 = (bf16[8,2048]{1,0:T(8,128)(2,1)S(1)}, bf16[8,2048]{1,0:T(8,128)(2,1)}, u32[]{:S(2)}) copy-start(bf16[8,2048]{1,0:T(8,128)(2,1)} %tokens_ref.1) | copy-start | bytes 98308
  1.6 6.4 %collective-permute-start = (bf16[8,2176]{1,0:T(8,128)(2,1)S(1)}, bf16[8,2176]{1,0:T(8,128)(2,1)S(1)}, u32[]{:S(2)}, u32[]{:S(2)}) collective-permute-start(bf16[8,2176]{1,0:T(8,128)(2,1)S(1)} %shard_map.73.after), channel_id=1, source_target_pairs={{0,8},{1,9},{2,10},{3,11},{4,12},{5,13},{6,14},{7,15},{8,0},{9,1},... | collective-permute-start | bytes 104456 | tf_op jit(solution)/shard_map/ppermute | solution.py:73
  5.7 1.9 %copy-start = (bf16[1,2048,768]{2,1,0:T(8,128)(2,1)S(1)}, bf16[1,2048,768]{2,1,0:T(8,128)(2,1)}, u32[]{:S(2)}) copy-start(bf16[1,2048,768]{2,1,0:T(8,128)(2,1)} %source.3) | copy-start | bytes 9437188
  7.6 5.5 %copy-start.1 = (bf16[1,768,2048]{2,1,0:T(8,128)(2,1)S(1)}, bf16[1,768,2048]{2,1,0:T(8,128)(2,1)}, u32[]{:S(2)}) copy-start(bf16[1,768,2048]{2,1,0:T(8,128)(2,1)} %source.5) | copy-start | bytes 9437188
  8.0 5.4 %copy-start.2 = (bf16[1,2048,768]{2,1,0:T(8,128)(2,1)S(1)}, bf16[1,2048,768]{2,1,0:T(8,128)(2,1)}, u32[]{:S(2)}) copy-start(bf16[1,2048,768]{2,1,0:T(8,128)(2,1)} %source.4) | copy-start | bytes 9437188
  8.0 5.1 %collective-permute-start.1 = (bf16[16,2176]{1,0:T(8,128)(2,1)S(1)}, bf16[16,2176]{1,0:T(8,128)(2,1)S(1)}, u32[]{:S(2)}, u32[]{:S(2)}) collective-permute-start(bf16[16,2176]{1,0:T(8,128)(2,1)S(1)} %pad_maximum_fusion.after.refs_0_), channel_id=1, source_target_pairs={{0,2},{1,3},{2,0},{3,1},{4,6},{5,7},{6,4},{7,5},{8,10},{9,11},{10,... | collective-permute-start | bytes 208904 | tf_op jit(solution)/shard_map/ppermute | solution.py:73
  9.7 5.2 %collective-permute-start.5 = (bf16[16,2176]{1,0:T(8,128)(2,1)S(1)}, bf16[16,2176]{1,0:T(8,128)(2,1)S(1)}, u32[]{:S(2)}, u32[]{:S(2)}) collective-permute-start(bf16[16,2176]{1,0:T(8,128)(2,1)S(1)} %pad_maximum_fusion.after.refs_0_), channel_id=1, source_target_pairs={{0,6},{1,7},{2,4},{3,5},{4,2},{5,3},{6,0},{7,1},{8,14},{9,15},{10,... | collective-permute-start | bytes 208904 | tf_op jit(solution)/shard_map/ppermute | solution.py:73
  11.0 3.9 %collective-permute-start.3 = (bf16[16,2176]{1,0:T(8,128)(2,1)S(1)}, bf16[16,2176]{1,0:T(8,128)(2,1)S(1)}, u32[]{:S(2)}, u32[]{:S(2)}) collective-permute-start(bf16[16,2176]{1,0:T(8,128)(2,1)S(1)} %pad_maximum_fusion.after.refs_0_), channel_id=1, source_target_pairs={{0,1},{1,0},{2,3},{3,2},{4,5},{5,4},{6,7},{7,6},{8,9},{9,8},{10,11... | collective-permute-start | bytes 208904 | tf_op jit(solution)/shard_map/ppermute | solution.py:73
  11.0 4.6 %collective-permute-start.2 = (bf16[16,2176]{1,0:T(8,128)(2,1)S(1)}, bf16[16,2176]{1,0:T(8,128)(2,1)S(1)}, u32[]{:S(2)}, u32[]{:S(2)}) collective-permute-start(bf16[16,2176]{1,0:T(8,128)(2,1)S(1)} %pad_maximum_fusion.after.refs_0_), channel_id=1, source_target_pairs={{0,4},{1,5},{2,6},{3,7},{4,0},{5,1},{6,2},{7,3},{8,12},{9,13},{10,... | collective-permute-start | bytes 208904 | tf_op jit(solution)/shard_map/ppermute | solution.py:73
  13.1 2.5 %collective-permute-start.4 = (bf16[16,2176]{1,0:T(8,128)(2,1)S(1)}, bf16[16,2176]{1,0:T(8,128)(2,1)S(1)}, u32[]{:S(2)}, u32[]{:S(2)}) collective-permute-start(bf16[16,2176]{1,0:T(8,128)(2,1)S(1)} %collective-permute-done.1.refs_1_), channel_id=1, source_target_pairs={{0,1},{1,0},{2,3},{3,2},{4,5},{5,4},{6,7},{7,6},{8,9},{9,8},{10,11... | collective-permute-start | bytes 208904 | tf_op jit(solution)/shard_map/ppermute | solution.py:73
  13.4 3.5 %copy-start.4 = (s32[1,6]{1,0:T(1,128)S(1)}, s32[1,6]{1,0:T(1,128)}, u32[]{:S(2)}) copy-start(s32[1,6]{1,0:T(1,128)} %refs_8_.1) | copy-start | bytes 76
  15.0 1.3 %collective-permute-start.7 = (bf16[16,2176]{1,0:T(8,128)(2,1)S(1)}, bf16[16,2176]{1,0:T(8,128)(2,1)S(1)}, u32[]{:S(2)}, u32[]{:S(2)}) collective-permute-start(bf16[16,2176]{1,0:T(8,128)(2,1)S(1)} %collective-permute-done.5.refs_3_), channel_id=1, source_target_pairs={{0,1},{1,0},{2,3},{3,2},{4,5},{5,4},{6,7},{7,6},{8,9},{9,8},{10,11... | collective-permute-start | bytes 208904 | tf_op jit(solution)/shard_map/ppermute | solution.py:73
  15.6 1.3 %collective-permute-start.6 = (bf16[16,2176]{1,0:T(8,128)(2,1)S(1)}, bf16[16,2176]{1,0:T(8,128)(2,1)S(1)}, u32[]{:S(2)}, u32[]{:S(2)}) collective-permute-start(bf16[16,2176]{1,0:T(8,128)(2,1)S(1)} %collective-permute-done.2.refs_2_), channel_id=1, source_target_pairs={{0,1},{1,0},{2,3},{3,2},{4,5},{5,4},{6,7},{7,6},{8,9},{9,8},{10,11... | collective-permute-start | bytes 208904 | tf_op jit(solution)/shard_map/ppermute | solution.py:73
  19.0 1.4 %collective-permute-start.8 = (bf16[32,2048]{1,0:T(8,128)(2,1)S(1)}, bf16[32,2048]{1,0:T(8,128)(2,1)S(1)}, u32[]{:S(2)}, u32[]{:S(2)}) collective-permute-start(bf16[32,2048]{1,0:T(8,128)(2,1)S(1)} %get-tuple-element.27), channel_id=1, source_target_pairs={{0,1},{1,0},{2,3},{3,2},{4,5},{5,4},{6,7},{7,6},{8,9},{9,8},{10,11... | collective-permute-start | bytes 393224 | tf_op jit(solution)/shard_map/ppermute | solution.py:73
  19.2 2.8 %collective-permute-start.10 = (bf16[16,2048]{1,0:T(8,128)(2,1)S(1)}, bf16[16,2048]{1,0:T(8,128)(2,1)S(1)}, u32[]{:S(2)}, u32[]{:S(2)}) collective-permute-start(bf16[16,2048]{1,0:T(8,128)(2,1)S(1)} %get-tuple-element.29), channel_id=1, source_target_pairs={{0,1},{1,0},{2,3},{3,2},{4,5},{5,4},{6,7},{7,6},{8,9},{9,8},{10,11... | collective-permute-start | bytes 196616 | tf_op jit(solution)/shard_map/ppermute | solution.py:73
  20.4 5.5 %collective-permute-start.9 = (bf16[32,2048]{1,0:T(8,128)(2,1)S(1)}, bf16[32,2048]{1,0:T(8,128)(2,1)S(1)}, u32[]{:S(2)}, u32[]{:S(2)}) collective-permute-start(bf16[32,2048]{1,0:T(8,128)(2,1)S(1)} %add_convert_fusion), channel_id=1, source_target_pairs={{0,2},{1,5},{2,0},{3,7},{4,6},{5,1},{6,4},{7,3},{8,10},{9,13},{10,... | collective-permute-start | bytes 393224 | tf_op jit(solution)/shard_map/ppermute | solution.py:77
  22.0 5.2 %collective-permute-start.11 = (bf16[16,2048]{1,0:T(8,128)(2,1)S(1)}, bf16[16,2048]{1,0:T(8,128)(2,1)S(1)}, u32[]{:S(2)}, u32[]{:S(2)}) collective-permute-start(bf16[16,2048]{1,0:T(8,128)(2,1)S(1)} %add_convert_fusion.2), channel_id=1, source_target_pairs={{0,6},{1,7},{2,4},{3,5},{4,2},{5,3},{6,0},{7,1},{8,14},{9,15},{10,... | collective-permute-start | bytes 196616 | tf_op jit(solution)/shard_map/ppermute | solution.py:73
  25.9 1.3 %collective-permute-start.12 = (bf16[16,2048]{1,0:T(8,128)(2,1)S(1)}, bf16[16,2048]{1,0:T(8,128)(2,1)S(1)}, u32[]{:S(2)}, u32[]{:S(2)}) collective-permute-start(bf16[16,2048]{1,0:T(8,128)(2,1)S(1)} %add_convert_fusion.1), channel_id=1, source_target_pairs={{0,1},{1,0},{2,3},{3,2},{4,5},{5,4},{6,7},{7,6},{8,9},{9,8},{10,11... | collective-permute-start | bytes 196616 | tf_op jit(solution)/shard_map/ppermute | solution.py:73
  27.3 4.9 %collective-permute-start.13 = (bf16[8,2048]{1,0:T(8,128)(2,1)S(1)}, bf16[8,2048]{1,0:T(8,128)(2,1)S(1)}, u32[]{:S(2)}, u32[]{:S(2)}) collective-permute-start(bf16[8,2048]{1,0:T(8,128)(2,1)S(1)} %add_convert_fusion.4), channel_id=1, source_target_pairs={{0,8},{1,9},{2,10},{3,11},{4,12},{5,13},{6,14},{7,15},{8,0},{9,1},... | collective-permute-start | bytes 98312 | tf_op jit(solution)/shard_map/ppermute | solution.py:73
